TPU v7x, 256 devices: a whole 4x4x8 slice. The times are simulated.
256 devices in a mesh: lang: 16 (over z_hi, x, core), seq: 16 (over y, z_lo).
Axes of the slice: x: 4, y: 4, z: 8 (z_hi: 2, z_lo: 4; z = z_hi * 4 + z_lo), core: 2. Of those that a mesh axis runs over, the one named last changes fastest.
Arguments:
- prompt_rows: bfloat16 [32768, 2048], P(('lang', 'seq')), may hold values from -6 to 6
- expert_ids: int32 [32768, 2], P(('lang', 'seq')), may hold values from 0 to 15, all different within a row; in each aligned block of 128 rows (0 to 127, 128 to 255, ...) at most 24 rows name the same one
- expert_gates: float32 [32768, 2], P(('lang', 'seq')), may hold values from 0.25 to 1
- w_gate: bfloat16 [16, 2048, 704], P('lang', 'seq'), may hold values from -0.125 to 0.125
- w_up: bfloat16 [16, 2048, 704], P('lang', 'seq'), may hold values from -0.125 to 0.125
- w_down: bfloat16 [16, 704, 2048], P('lang', None, 'seq'), may hold values from -0.21875 to 0.21875
- w_kv: bfloat16 [2048, 2, 2048], P(None, None, 'seq'), may hold values from -0.125 to 0.125
- prompt_lengths: int32 [32], P('lang'), may hold values from 256 to 1024, as said below
- latent_q: bfloat16 [32, 1024, 2048], P('lang', 'seq'), may hold values from -5 to 5
- latent_k: bfloat16 [32, 1024, 2048], P('lang', 'seq'), may hold values from -5 to 5
- latent_v: bfloat16 [32, 1024, 2048], P('lang', 'seq'), may hold values from -6 to 6
- grad_out: bfloat16 [32, 1024, 2048], P('lang', 'seq'), may hold values from -6 to 6
Outputs:
- attended: bfloat16 [32, 1024, 2048], P('lang', 'seq')
- grad_latent: bfloat16 [3, 32, 1024, 2048], P(None, 'lang', 'seq')
- grad_wkv: float32 [2048, 2, 2048], P(None, None, 'seq')
Inputs may be any that keep to these rules, and one draw needn't show every extreme that they name: `expert_ids`: in each aligned block of 128 rows (the rows of one device) no expert is named by more than 24 rows. `prompt_lengths`: the first of each group of 2 pages uses its whole prompt.
All inputs are finite; a program needn't handle non-finite values.
Results may differ from a plain program's by a relative error of at most 0.03.
Values may be sent and summed in bfloat16 or wider, within the bound.
A program may use at most 128 MiB of HBM per device.

v0:
```python
import math

import jax
import jax.numpy as jnp
from jax import lax
from jax.sharding import PartitionSpec as P

HD = 128


def joint_attention(queries, key_rows, values, key_valid, out_grads):
    rows_all, head_size = queries.shape
    block_rows = min(512, rows_all)
    blocks = rows_all // block_rows
    score_scale = 1.0 / math.sqrt(head_size)
    query_blocks = queries.reshape(blocks, block_rows, head_size)
    grad_blocks = out_grads.reshape(blocks, block_rows, head_size)

    def one_block(carry, inputs):
        key_grad, value_grad = carry
        query_block, grad_block = inputs
        scores = (
            lax.dot_general(
                query_block, key_rows, (((1,), (1,)), ((), ())), preferred_element_type=jnp.float32
            )
            * score_scale
        )
        scores = jnp.where(key_valid[None, :], scores, -jnp.inf)
        highest = jnp.max(scores, axis=1, keepdims=True)
        raised = jnp.exp(scores - highest)
        soft_weights = raised / jnp.sum(raised, axis=1, keepdims=True)
        soft_low = soft_weights.astype(jnp.bfloat16)
        attended = jnp.dot(soft_low, values, preferred_element_type=jnp.float32).astype(
            jnp.bfloat16
        )
        prob_grad = lax.dot_general(
            grad_block, values, (((1,), (1,)), ((), ())), preferred_element_type=jnp.float32
        )
        centre = jnp.sum(soft_weights * prob_grad, axis=1, keepdims=True)
        score_grad = (soft_weights * (prob_grad - centre) * score_scale).astype(jnp.bfloat16)
        query_grad = jnp.dot(score_grad, key_rows, preferred_element_type=jnp.float32).astype(
            jnp.bfloat16
        )
        key_grad = key_grad + lax.dot_general(
            score_grad, query_block, (((0,), (0,)), ((), ())), preferred_element_type=jnp.float32
        )
        value_grad = value_grad + lax.dot_general(
            soft_low, grad_block, (((0,), (0,)), ((), ())), preferred_element_type=jnp.float32
        )
        return ((key_grad, value_grad), (attended, query_grad))

    empty_grad = jnp.zeros(key_rows.shape, jnp.float32)
    (key_grad, value_grad), (attended, query_grad) = lax.scan(
        one_block, (empty_grad, empty_grad), (query_blocks, grad_blocks)
    )
    return (
        attended.reshape(rows_all, head_size),
        query_grad.reshape(rows_all, head_size),
        key_grad,
        value_grad,
    )


def slot_targets(expert_ids, experts_all, capacity):
    rows_local, picks = expert_ids.shape
    flat_ids = expert_ids.reshape(rows_local * picks)
    expert_range = jnp.arange(experts_all, dtype=jnp.int32)
    onehot = (flat_ids[:, None] == expert_range[None, :]).astype(jnp.int32)
    earlier = jnp.cumsum(onehot, axis=0) - onehot
    slot_index = jnp.sum(earlier * onehot, axis=1)
    return (flat_ids * capacity + slot_index).reshape(rows_local, picks)


def to_heads(latent_q, latent_k, latent_v, grad_out):
    return (
        lax.all_to_all(latent_q, "seq", split_axis=2, concat_axis=1, tiled=True),
        lax.all_to_all(latent_k, "seq", split_axis=2, concat_axis=1, tiled=True),
        lax.all_to_all(latent_v, "seq", split_axis=2, concat_axis=1, tiled=True),
        lax.all_to_all(grad_out, "seq", split_axis=2, concat_axis=1, tiled=True),
    )


def local(
    prompt_rows,
    expert_ids,
    expert_gates,
    w_gate,
    w_up,
    w_down,
    w_kv,
    prompt_lengths,
    latent_q,
    latent_k,
    latent_v,
    grad_out,
):
    lang_count = lax.axis_size("lang")
    exp_local = w_gate.shape[0]
    experts_all = lang_count * exp_local
    rows_local, model_width = prompt_rows.shape
    capacity = 3 * rows_local // experts_all
    targets = slot_targets(expert_ids, experts_all, capacity)
    slot_ids = jnp.arange(experts_all * capacity, dtype=jnp.int32)
    dispatch_mask = jnp.any(slot_ids[:, None, None] == targets[None, :, :], axis=2).astype(
        jnp.bfloat16
    )
    outgoing = jnp.dot(dispatch_mask, prompt_rows, preferred_element_type=jnp.float32).astype(
        jnp.bfloat16
    )
    outgoing = outgoing.reshape(experts_all, capacity, model_width)
    arrived = lax.all_to_all(outgoing, "lang", split_axis=0, concat_axis=1, tiled=True)
    gate_sum = jnp.einsum(
        "erd,edf->erf",
        arrived,
        lax.all_gather(w_gate, "seq", axis=1, tiled=True),
        preferred_element_type=jnp.float32,
    )
    up_sum = jnp.einsum(
        "erd,edf->erf",
        arrived,
        lax.all_gather(w_up, "seq", axis=1, tiled=True),
        preferred_element_type=jnp.float32,
    )
    hidden = (jax.nn.silu(gate_sum) * up_sum).astype(jnp.bfloat16)
    expert_result = jnp.einsum(
        "erf,efd->erd",
        hidden,
        lax.all_gather(w_down, "seq", axis=2, tiled=True),
        preferred_element_type=jnp.float32,
    ).astype(jnp.bfloat16)
    returned = lax.all_to_all(
        expert_result, "lang", split_axis=1, concat_axis=0, tiled=True
    ).reshape(experts_all * capacity, model_width)
    mixed_sum = jnp.zeros((rows_local, model_width), jnp.float32)
    for which in range(targets.shape[1]):
        picker = (targets[:, which][:, None] == slot_ids[None, :]).astype(jnp.bfloat16)
        picked = jnp.dot(picker, returned, preferred_element_type=jnp.float32)
        mixed_sum = mixed_sum + expert_gates[:, which][:, None] * picked
    mixed = mixed_sum.astype(jnp.bfloat16)
    group_rows = lax.all_gather(mixed, "seq", axis=0, tiled=True)
    page_count = prompt_lengths.shape[0]
    prompt_len = group_rows.shape[0] // page_count
    heads_local = w_kv.shape[2] // HD
    kv_local = jnp.dot(
        group_rows,
        w_kv.reshape(model_width, 2 * heads_local * HD),
        preferred_element_type=jnp.float32,
    ).astype(jnp.bfloat16)
    kv_local = kv_local.reshape(page_count, prompt_len, 2, heads_local, HD)
    head_layout = to_heads(latent_q, latent_k, latent_v, grad_out)
    query_heads, key_heads, value_heads, grad_heads = head_layout
    lat_len = query_heads.shape[1]

    def split_heads(array):
        return (
            array.reshape(page_count, lat_len, heads_local, HD)
            .transpose(0, 2, 1, 3)
            .reshape(page_count * heads_local, lat_len, HD)
        )

    def prompt_part(index):
        return (
            kv_local[:, :, index]
            .transpose(0, 2, 1, 3)
            .reshape(page_count * heads_local, prompt_len, HD)
        )

    positions = jnp.arange(prompt_len, dtype=jnp.int32)
    prompt_valid = positions[None, :] < prompt_lengths[:, None]
    key_valid = jnp.concatenate([jnp.ones((page_count, lat_len), bool), prompt_valid], axis=1)
    key_valid = jnp.repeat(key_valid, heads_local, axis=0)

    def one_item(inputs):
        query_item, key_item, value_item, grad_item, prompt_key, prompt_value, valid_item = inputs
        key_rows = jnp.concatenate([key_item, prompt_key], axis=0)
        value_rows = jnp.concatenate([value_item, prompt_value], axis=0)
        return joint_attention(query_item, key_rows, value_rows, valid_item, grad_item)

    attended, query_grad, key_grad, value_grad = lax.map(
        one_item,
        (
            split_heads(query_heads),
            split_heads(key_heads),
            split_heads(value_heads),
            split_heads(grad_heads),
            prompt_part(0),
            prompt_part(1),
            key_valid,
        ),
    )

    def join_heads(array):
        return (
            array.reshape(page_count, heads_local, lat_len, HD)
            .transpose(0, 2, 1, 3)
            .reshape(page_count, lat_len, heads_local * HD)
        )

    latent_key = key_grad[:, :lat_len].astype(jnp.bfloat16)
    latent_value = value_grad[:, :lat_len].astype(jnp.bfloat16)
    attended_rows, query_rows, key_rows_back, value_rows_back = (
        lax.all_to_all(join_heads(attended), "seq", split_axis=1, concat_axis=2, tiled=True),
        lax.all_to_all(join_heads(query_grad), "seq", split_axis=1, concat_axis=2, tiled=True),
        lax.all_to_all(join_heads(latent_key), "seq", split_axis=1, concat_axis=2, tiled=True),
        lax.all_to_all(join_heads(latent_value), "seq", split_axis=1, concat_axis=2, tiled=True),
    )
    grad_latent = jnp.stack([query_rows, key_rows_back, value_rows_back])

    def prompt_back(array):
        return (
            array[:, lat_len:]
            .astype(jnp.bfloat16)
            .reshape(page_count, heads_local, prompt_len, HD)
            .transpose(0, 2, 1, 3)
        )

    prompt_grad = jnp.stack([prompt_back(key_grad), prompt_back(value_grad)], axis=2).reshape(
        page_count * prompt_len, 2 * heads_local * HD
    )
    partial_grad = lax.dot_general(
        group_rows, prompt_grad, (((0,), (0,)), ((), ())), preferred_element_type=jnp.float32
    )
    grad_wkv = (
        lax.psum(partial_grad.astype(jnp.bfloat16), "lang")
        .astype(jnp.float32)
        .reshape(model_width, 2, heads_local * HD)
    )
    return (attended_rows, grad_latent, grad_wkv)


def solution(mesh):
    return jax.shard_map(
        local,
        mesh=mesh,
        in_specs=(
            P(("lang", "seq"), None),
            P(("lang", "seq"), None),
            P(("lang", "seq"), None),
            P("lang", "seq", None),
            P("lang", "seq", None),
            P("lang", None, "seq"),
            P(None, None, "seq"),
            P("lang"),
            P("lang", "seq", None),
            P("lang", "seq", None),
            P("lang", "seq", None),
            P("lang", "seq", None),
        ),
        out_specs=(P("lang", "seq", None), P(None, "lang", "seq", None), P(None, None, "seq")),
        check_vma=False,
    )
```

profile of v0, /device:TPU:1, one launch (start us, length us, event | category | flops | bytes accessed | tf_op | source)
XLA Modules:
  0.0 1074.1 jit_solution(5428050211046339989)
XLA Ops:
  12.9 67.4 %all_to_all.153 = bf16[16,24,2048]{2,1,0:T(8,128)(2,1)S(1)} all-to-all(bf16[16,24,2048]{2,1,0:T(8,128)(2,1)S(1)} %bitcast.229), channel_id=1, replica_groups=mesh['lang'=16,'seq'=16] {'lang'}, dimensions={0} | all-to-all | bytes 3145728 | tf_op jit(solution)/shard_map/all_to_all | solution.py:111
  80.4 47.8 %all-gather.5.cloned.1.call-done = bf16[1,2048,704]{1,2,0:T(8,128)(2,1)} async-done(((bf16[1,128,704]{1,2,0:T(8,128)(2,1)}), bf16[1,2048,704]{1,2,0:T(8,128)(2,1)}) %all-gather.5.cloned.1.call-update) | async-done | bytes 2883600 | tf_op jit(solution)/shard_map/all_gather | solution.py:115
  131.7 91.0 %all-gather.7.cloned.1.call-done = bf16[1,2048,704]{1,2,0:T(8,128)(2,1)} async-done(((bf16[1,128,704]{1,2,0:T(8,128)(2,1)}), bf16[1,2048,704]{1,2,0:T(8,128)(2,1)}) %all-gather.7.cloned.1.call-update) | async-done | bytes 2883600 | tf_op jit(solution)/shard_map/all_gather | solution.py:121
  222.6 93.7 %all-gather.9.cloned.1.call-done = bf16[1,704,2048]{2,1,0:T(8,128)(2,1)} async-done(((bf16[1,704,128]{2,1,0:T(8,128)(2,1)}), bf16[1,704,2048]{2,1,0:T(8,128)(2,1)}) %all-gather.9.cloned.1.call-update) | async-done | bytes 2883600 | tf_op jit(solution)/shard_map/all_gather | solution.py:128
  327.6 11.3 %reduce.4 = bf16[384,2048]{1,0:T(8,128)(2,1)} reduce(bf16[384,1,2048]{2,1,0:T(2,128)(2,1)S(1)} %bitcast.224, bf16[]{:T(256)} %broadcast.71), dimensions={1}, to_apply=%bitcast.176.reduce_sub_computation | reduce | bytes 3145730
  343.8 14.6 %all-to-all-start.4 = ((bf16[16,2,24576]{2,1,0:T(2,128)(2,1)}), bf16[16,2,24576]{2,1,0:T(2,128)(2,1)}, u32[]{:S(2)}, u32[]{:S(2)}) async-start(bf16[16,2,24576]{2,1,0:T(2,128)(2,1)} %reshape.128), calls=%async_computation.4 | async-start | bytes 3145728 | tf_op jit(solution)/shard_map/all_to_all | solution.py:131
  358.5 25.4 %all-to-all-done.4 = bf16[16,2,24576]{2,1,0:T(2,128)(2,1)} async-done(((bf16[16,2,24576]{2,1,0:T(2,128)(2,1)}), bf16[16,2,24576]{2,1,0:T(2,128)(2,1)}, u32[]{:S(2)}, u32[]{:S(2)}) %all-to-all-start.4) | async-done | bytes 1572896 | tf_op jit(solution)/shard_map/all_to_all | solution.py:131
  399.1 22.2 %all-to-all-start = ((bf16[16,2,8192]{2,1,0:T(2,128)(2,1)}), bf16[16,2,8192]{2,1,0:T(2,128)(2,1)S(1)}, u32[]{:S(2)}, u32[]{:S(2)}) async-start(bf16[16,2,8192]{2,1,0:T(2,128)(2,1)} %reshape.122), calls=%async_computation | async-start | bytes 1048576 | tf_op jit(solution)/shard_map/all_to_all | solution.py:76
  423.6 28.3 %all-to-all-done = bf16[16,2,8192]{2,1,0:T(2,128)(2,1)S(1)} async-done(((bf16[16,2,8192]{2,1,0:T(2,128)(2,1)}), bf16[16,2,8192]{2,1,0:T(2,128)(2,1)S(1)}, u32[]{:S(2)}, u32[]{:S(2)}) %all-to-all-start) | async-done | bytes 524320 | tf_op jit(solution)/shard_map/all_to_all | solution.py:76
  457.8 28.5 %all-to-all-done.1 = bf16[16,2,8192]{2,1,0:T(2,128)(2,1)S(1)} async-done(((bf16[16,2,8192]{2,1,0:T(2,128)(2,1)}), bf16[16,2,8192]{2,1,0:T(2,128)(2,1)S(1)}, u32[]{:S(2)}, u32[]{:S(2)}) %all-to-all-start.1) | async-done | bytes 524320 | tf_op jit(solution)/shard_map/all_to_all | solution.py:79
  492.2 28.4 %all-to-all-done.2 = bf16[16,2,8192]{2,1,0:T(2,128)(2,1)S(1)} async-done(((bf16[16,2,8192]{2,1,0:T(2,128)(2,1)}), bf16[16,2,8192]{2,1,0:T(2,128)(2,1)S(1)}, u32[]{:S(2)}, u32[]{:S(2)}) %all-to-all-start.2) | async-done | bytes 524320 | tf_op jit(solution)/shard_map/all_to_all | solution.py:77
  520.5 15.7 %all-to-all-start.5 = ((bf16[16,2,8192]{2,1,0:T(2,128)(2,1)}), bf16[16,2,8192]{2,1,0:T(2,128)(2,1)S(1)}, u32[]{:S(2)}, u32[]{:S(2)}) async-start(bf16[16,2,8192]{2,1,0:T(2,128)(2,1)} %reshape.130), calls=%async_computation.5 | async-start | bytes 1048576 | tf_op jit(solution)/shard_map/all_to_all | solution.py:78
  540.7 25.9 %all-to-all-done.5 = bf16[16,2,8192]{2,1,0:T(2,128)(2,1)S(1)} async-done(((bf16[16,2,8192]{2,1,0:T(2,128)(2,1)}), bf16[16,2,8192]{2,1,0:T(2,128)(2,1)S(1)}, u32[]{:S(2)}, u32[]{:S(2)}) %all-to-all-start.5) | async-done | bytes 524320 | tf_op jit(solution)/shard_map/all_to_all | solution.py:78
  568.0 67.2 %all-gather.11.cloned.1.call-done = bf16[2048,2048]{1,0:T(8,128)(2,1)} async-done(((bf16[128,2048]{1,0:T(8,128)(2,1)}), bf16[2048,2048]{1,0:T(8,128)(2,1)}) %all-gather.11.cloned.1.call-update) | async-done | bytes 8388624 | tf_op jit(solution)/shard_map/all_gather | solution.py:140
  645.2 160.9 %while.34 = (s32[]{:T(128)}, bf16[2,1024,128]{2,1,0:T(8,128)(2,1)}, bf16[2,1024,128]{2,1,0:T(8,128)(2,1)}, bf16[2,2048,128]{2,0,1:T(2,128)(2,1)}, bf16[2,2048,12...) while((s32[]{:T(128)}, bf16[2,1024,128]{2,1,0:T(8,128)(2,1)}, ...), condition=%wide.region_10.11_spmd, body=%wide.region_4.10_spmd.sunk | while | flops 1633810944 | bytes 130837520 | solution.py:179
  646.9 27.6 %while.35 = (s32[]{:T(128)}, f32[2048,128]{1,0:T(8,128)S(1)}, f32[2048,128]{1,0:T(8,128)}, bf16[2,512,128]{2,1,0:T(8,128)(2,1)}, bf16[2,512,128]{2,1,0:T(8,128)(...) while((s32[]{:T(128)}, f32[2048,128]{1,0:T(8,128)S(1)}, ...), condition=%wide.region_9.9_spmd.clone, body=%wide.region_5.8_spmd.clone.sunk | while | flops 1631713792 | bytes 95180672 | solution.py:53
  674.5 24.5 %dynamic_update_slice.33 = bf16[2,2048,128]{2,0,1:T(2,128)(2,1)} dynamic-update-slice(bf16[2,2048,128]{2,0,1:T(2,128)(2,1)} %get-tuple-element.455, f32[1,2048,128]{2,0,1:T(1,128)S(1)} %bitcast.219, s32[]{:T(128)} %get-tuple-element.452, s32[]{:T(128)} %constant.54.clone.1..sunk, s32[]{:T(128)} %constant.54.clone.1..sunk) | dynamic-update-slice | bytes 2097156 | tf_op jit(solution)/shard_map/while/body/jit(dynamic_update_index_in_dim)/dynamic_update_slice | solution.py:179
  699.0 24.8 %dynamic_update_slice.34 = bf16[2,2048,128]{2,0,1:T(2,128)(2,1)} dynamic-update-slice(bf16[2,2048,128]{2,0,1:T(2,128)(2,1)} %get-tuple-element.456, f32[1,2048,128]{2,0,1:T(1,128)} %bitcast.206, s32[]{:T(128)} %get-tuple-element.452, s32[]{:T(128)} %constant.54.clone.1..sunk, s32[]{:T(128)} %constant.54.clone.1..sunk) | dynamic-update-slice | bytes 2097156 | tf_op jit(solution)/shard_map/while/body/jit(dynamic_update_index_in_dim)/dynamic_update_slice | solution.py:179
  727.3 27.6 %while.35 = (s32[]{:T(128)}, f32[2048,128]{1,0:T(8,128)S(1)}, f32[2048,128]{1,0:T(8,128)}, bf16[2,512,128]{2,1,0:T(8,128)(2,1)}, bf16[2,512,128]{2,1,0:T(8,128)(...) while((s32[]{:T(128)}, f32[2048,128]{1,0:T(8,128)S(1)}, ...), condition=%wide.region_9.9_spmd.clone, body=%wide.region_5.8_spmd.clone.sunk | while | flops 1631713792 | bytes 95180672 | solution.py:53
  754.9 24.5 %dynamic_update_slice.33 = bf16[2,2048,128]{2,0,1:T(2,128)(2,1)} dynamic-update-slice(bf16[2,2048,128]{2,0,1:T(2,128)(2,1)} %get-tuple-element.455, f32[1,2048,128]{2,0,1:T(1,128)S(1)} %bitcast.219, s32[]{:T(128)} %get-tuple-element.452, s32[]{:T(128)} %constant.54.clone.1..sunk, s32[]{:T(128)} %constant.54.clone.1..sunk) | dynamic-update-slice | bytes 2097156 | tf_op jit(solution)/shard_map/while/body/jit(dynamic_update_index_in_dim)/dynamic_update_slice | solution.py:179
  779.5 24.8 %dynamic_update_slice.34 = bf16[2,2048,128]{2,0,1:T(2,128)(2,1)} dynamic-update-slice(bf16[2,2048,128]{2,0,1:T(2,128)(2,1)} %get-tuple-element.456, f32[1,2048,128]{2,0,1:T(1,128)} %bitcast.206, s32[]{:T(128)} %get-tuple-element.452, s32[]{:T(128)} %constant.54.clone.1..sunk, s32[]{:T(128)} %constant.54.clone.1..sunk) | dynamic-update-slice | bytes 2097156 | tf_op jit(solution)/shard_map/while/body/jit(dynamic_update_index_in_dim)/dynamic_update_slice | solution.py:179
  817.6 14.2 %all-to-all-done.8 = bf16[2,1024,128]{2,0,1:T(2,128)(2,1)S(1)} async-done(((bf16[2,1024,128]{2,0,1:T(2,128)(2,1)}), bf16[2,1024,128]{2,0,1:T(2,128)(2,1)S(1)}, u32[]{:S(2)}, u32[]{:S(2)}) %all-to-all-start.8) | async-done | bytes 524320 | tf_op jit(solution)/shard_map/all_to_all | solution.py:204
  836.7 14.3 %all-to-all-done.9 = bf16[2,1024,128]{2,0,1:T(2,128)(2,1)S(1)} async-done(((bf16[2,1024,128]{2,0,1:T(2,128)(2,1)}), bf16[2,1024,128]{2,0,1:T(2,128)(2,1)S(1)}, u32[]{:S(2)}, u32[]{:S(2)}) %all-to-all-start.9) | async-done | bytes 524320 | tf_op jit(solution)/shard_map/all_to_all | solution.py:205
  892.4 172.1 %all-reduce.3.cloned.1.call-done = bf16[2048,2,128]{2,1,0:T(2,128)(2,1)} async-done(((bf16[2048,2,128]{2,1,0:T(2,128)(2,1)}), bf16[2048,2,128]{2,1,0:T(2,128)(2,1)}) %all-reduce.3.cloned.1.call-update) | async-done | bytes 1048592 | tf_op jit(solution)/shard_map/psum | solution.py:224
  (276 shorter events, 192.2 us)
Async XLA Ops:
  7.2 121.0 %all-gather.5.cloned.1.call-start = ((), (), s32[]{:S(2)}) async-start(), calls=%async_computation.10 | async-start | bytes 3063808 | tf_op jit(solution)/shard_map/all_gather | solution.py:115
  7.9 214.7 %all-gather.7.cloned.1.call-start = ((), (), s32[]{:S(2)}) async-start(), calls=%async_computation.11 | async-start | bytes 3063808 | tf_op jit(solution)/shard_map/all_gather | solution.py:121
  8.7 307.7 %all-gather.9.cloned.1.call-start = ((), (), s32[]{:S(2)}) async-start(), calls=%async_computation.12 | async-start | bytes 3063808 | tf_op jit(solution)/shard_map/all_gather | solution.py:128
  343.8 40.1 %all-to-all-start.4 = ((bf16[16,2,24576]{2,1,0:T(2,128)(2,1)}), bf16[16,2,24576]{2,1,0:T(2,128)(2,1)}, u32[]{:S(2)}, u32[]{:S(2)}) async-start(bf16[16,2,24576]{2,1,0:T(2,128)(2,1)} %reshape.128), calls=%async_computation.4 | async-start | bytes 3145728 | tf_op jit(solution)/shard_map/all_to_all | solution.py:131
  358.4 276.8 %all-gather.11.cloned.1.call-start = ((), (), s32[]{:S(2)}) async-start(), calls=%async_computation.13 | async-start | bytes 8912896 | tf_op jit(solution)/shard_map/all_gather | solution.py:140
  399.1 56.4 %copy-start.24 = (bf16[2,64,2048]{2,1,0:T(8,128)(2,1)S(1)}, bf16[2,64,2048]{2,1,0:T(8,128)(2,1)}, u32[]{:S(2)}) copy-start(bf16[2,64,2048]{2,1,0:T(8,128)(2,1)} %param.25) | copy-start | bytes 1572868
  399.1 52.8 %all-to-all-start = ((bf16[16,2,8192]{2,1,0:T(2,128)(2,1)}), bf16[16,2,8192]{2,1,0:T(2,128)(2,1)S(1)}, u32[]{:S(2)}, u32[]{:S(2)}) async-start(bf16[16,2,8192]{2,1,0:T(2,128)(2,1)} %reshape.122), calls=%async_computation | async-start | bytes 1048576 | tf_op jit(solution)/shard_map/all_to_all | solution.py:76
  423.6 66.3 %copy-start.25 = (bf16[2,64,2048]{2,1,0:T(8,128)(2,1)S(1)}, bf16[2,64,2048]{2,1,0:T(8,128)(2,1)}, u32[]{:S(2)}) copy-start(bf16[2,64,2048]{2,1,0:T(8,128)(2,1)} %param.26) | copy-start | bytes 1572868
  451.9 34.4 %all-to-all-start.1 = ((bf16[16,2,8192]{2,1,0:T(2,128)(2,1)}), bf16[16,2,8192]{2,1,0:T(2,128)(2,1)S(1)}, u32[]{:S(2)}, u32[]{:S(2)}) async-start(bf16[16,2,8192]{2,1,0:T(2,128)(2,1)} %reshape.124), calls=%async_computation.1 | async-start | bytes 1048576 | tf_op jit(solution)/shard_map/all_to_all | solution.py:79
  457.8 78.5 %copy-start.28 = (s32[2]{0:T(128)S(1)}, s32[2]{0:T(128)}, u32[]{:S(2)}) copy-start(s32[2]{0:T(128)} %param.23) | copy-start | bytes 28
  486.3 34.2 %all-to-all-start.2 = ((bf16[16,2,8192]{2,1,0:T(2,128)(2,1)}), bf16[16,2,8192]{2,1,0:T(2,128)(2,1)S(1)}, u32[]{:S(2)}, u32[]{:S(2)}) async-start(bf16[16,2,8192]{2,1,0:T(2,128)(2,1)} %reshape.126), calls=%async_computation.2 | async-start | bytes 1048576 | tf_op jit(solution)/shard_map/all_to_all | solution.py:77
  520.5 46.1 %all-to-all-start.5 = ((bf16[16,2,8192]{2,1,0:T(2,128)(2,1)}), bf16[16,2,8192]{2,1,0:T(2,128)(2,1)S(1)}, u32[]{:S(2)}, u32[]{:S(2)}) async-start(bf16[16,2,8192]{2,1,0:T(2,128)(2,1)} %reshape.130), calls=%async_computation.5 | async-start | bytes 1048576 | tf_op jit(solution)/shard_map/all_to_all | solution.py:78
  674.4 51.2 %copy-start.11 = (bf16[2,1024,128]{2,1,0:T(8,128)(2,1)S(1)}, bf16[2,1024,128]{2,1,0:T(8,128)(2,1)}, u32[]{:S(2)}) copy-start(bf16[2,1024,128]{2,1,0:T(8,128)(2,1)} %copy-done.10) | copy-start | bytes 1572868 | tf_op jit(solution)/shard_map/while
  674.4 51.2 %copy-start.13 = (bf16[2,1024,128]{2,1,0:T(8,128)(2,1)S(1)}, bf16[2,1024,128]{2,1,0:T(8,128)(2,1)}, u32[]{:S(2)}) copy-start(bf16[2,1024,128]{2,1,0:T(8,128)(2,1)} %copy-done.12) | copy-start | bytes 1572868 | tf_op jit(solution)/shard_map/while
  674.4 51.2 %copy-start.19 = (bf16[2,1024,128]{2,1,0:T(8,128)(2,1)S(1)}, bf16[2,1024,128]{2,1,0:T(8,128)(2,1)}, u32[]{:S(2)}) copy-start(bf16[2,1024,128]{2,1,0:T(8,128)(2,1)} %copy-done.18) | copy-start | bytes 1572868 | tf_op jit(solution)/shard_map/while
  754.9 51.2 %copy-start.11 = (bf16[2,1024,128]{2,1,0:T(8,128)(2,1)S(1)}, bf16[2,1024,128]{2,1,0:T(8,128)(2,1)}, u32[]{:S(2)}) copy-start(bf16[2,1024,128]{2,1,0:T(8,128)(2,1)} %copy-done.10) | copy-start | bytes 1572868 | tf_op jit(solution)/shard_map/while
  754.9 51.2 %copy-start.13 = (bf16[2,1024,128]{2,1,0:T(8,128)(2,1)S(1)}, bf16[2,1024,128]{2,1,0:T(8,128)(2,1)}, u32[]{:S(2)}) copy-start(bf16[2,1024,128]{2,1,0:T(8,128)(2,1)} %copy-done.12) | copy-start | bytes 1572868 | tf_op jit(solution)/shard_map/while
  754.9 51.2 %copy-start.19 = (bf16[2,1024,128]{2,1,0:T(8,128)(2,1)S(1)}, bf16[2,1024,128]{2,1,0:T(8,128)(2,1)}, u32[]{:S(2)}) copy-start(bf16[2,1024,128]{2,1,0:T(8,128)(2,1)} %copy-done.18) | copy-start | bytes 1572868 | tf_op jit(solution)/shard_map/while
  809.1 22.8 %all-to-all-start.8 = ((bf16[2,1024,128]{2,0,1:T(2,128)(2,1)}), bf16[2,1024,128]{2,0,1:T(2,128)(2,1)S(1)}, u32[]{:S(2)}, u32[]{:S(2)}) async-start(bf16[2,1024,128]{2,0,1:T(2,128)(2,1)} %get-tuple-element.212), calls=%async_computation.8 | async-start | bytes 1048576 | tf_op jit(solution)/shard_map/all_to_all | solution.py:204
  831.8 19.2 %all-to-all-start.9 = ((bf16[2,1024,128]{2,0,1:T(2,128)(2,1)}), bf16[2,1024,128]{2,0,1:T(2,128)(2,1)S(1)}, u32[]{:S(2)}, u32[]{:S(2)}) async-start(bf16[2,1024,128]{2,0,1:T(2,128)(2,1)} %get-tuple-element.214), calls=%async_computation.9 | async-start | bytes 1048576 | tf_op jit(solution)/shard_map/all_to_all | solution.py:205
  851.0 19.4 %all-to-all-start.7 = ((bf16[2,1024,128]{2,0,1:T(2,128)(2,1)}), bf16[2,1024,128]{2,0,1:T(2,128)(2,1)S(1)}, u32[]{:S(2)}, u32[]{:S(2)}) async-start(bf16[2,1024,128]{2,0,1:T(2,128)(2,1)} %copy.157), calls=%async_computation.7 | async-start | bytes 1048576 | tf_op jit(solution)/shard_map/all_to_all | solution.py:203
  870.5 19.2 %all-to-all-start.6 = ((bf16[2,1024,128]{2,0,1:T(2,128)(2,1)}), bf16[2,1024,128]{2,0,1:T(2,128)(2,1)S(1)}, u32[]{:S(2)}, u32[]{:S(2)}) async-start(bf16[2,1024,128]{2,0,1:T(2,128)(2,1)} %copy.155), calls=%async_computation.6 | async-start | bytes 1048576 | tf_op jit(solution)/shard_map/all_to_all | solution.py:202
  874.1 190.4 %all-reduce.3.cloned.1.call-start = ((), (), s32[]{:S(2)}) async-start(), calls=%async_computation.14 | async-start | bytes 2097152 | tf_op jit(solution)/shard_map/psum | solution.py:224
  890.1 177.2 %copy-start.1 = (bf16[128,2048]{1,0:T(8,128)(2,1)S(1)}, bf16[128,2048]{1,0:T(8,128)(2,1)}, u32[]{:S(2)}) copy-start(bf16[128,2048]{1,0:T(8,128)(2,1)} %param.16) | copy-start | bytes 1572868
  (55 other events, 392.0 us)
Sparse Core Ops, SparseCore 0:
  9.7 118.4 all-gather.4
  129.9 92.7 all-gather.6
  224.4 91.9 all-gather.8
  395.3 239.9 all-gather.10
  884.6 179.7 all-reduce.2
where the time goes:
time: 1100 us; the launch traced here: 1070 us
  waiting for transfers between devices  653 us (59%)
  local copies, waits for them, and re-layouts  168 us (15%)
  starting transfers between devices  77.8 us (7%)
  matrix products  68.5 us (6%)
  blocking collectives  67.4 us (6%)
  other arithmetic  24.4 us (2%)
  between operations  14.6 us (1%)
    psum x1, waiting for transfers between devices, local(): lax.psum(partial_grad.astype(jnp.bfloat16), 'lang').astype(jnp.float32)  172 us
    dynamic_update_slice x6, local copies, waits for them, and re-layouts, local(): lax.map(one_item, (split_heads(query_heads), split_heads(key_heads), spli...  102 us
    all_gather x1, waiting for transfers between devices, local(): lax.all_gather(w_down, 'seq', axis=2, tiled=True)  93.7 us
    all_gather x1, waiting for transfers between devices, local(): lax.all_gather(w_up, 'seq', axis=1, tiled=True)  91 us
    all_to_all x1, blocking collectives, local(): lax.all_to_all(outgoing, 'lang', split_axis=0, concat_axis=1, tiled=True)  67.4 us
    all_gather x1, waiting for transfers between devices, local(): group_rows = lax.all_gather(mixed, 'seq', axis=0, tiled=True)  67.2 us
    all_gather x1, waiting for transfers between devices, local(): lax.all_gather(w_gate, 'seq', axis=1, tiled=True)  47.8 us
    all_to_all x1, waiting for transfers between devices, to_heads(): lax.all_to_all(grad_out, 'seq', split_axis=2, concat_axis=1, tiled=True)  28.5 us
  transfers between devices with their start and end apart: 14, of which 14 were waited for; matrix products, arithmetic and copies ran while one was open for 4% of the time, Pallas kernels for 0%

commit v1 on v0

v1 whole, which is shorter than its diff:
```python
import functools
import math

import jax
import jax.numpy as jnp
from jax import lax
from jax.experimental import pallas as pl
from jax.experimental.pallas import tpu as pltpu
from jax.sharding import PartitionSpec as P

HD = 128
MESH = pl.DeviceIdType.MESH
ANY = pl.BlockSpec(memory_space=pl.ANY)
BF = jnp.bfloat16
F32 = jnp.float32
DMA = pltpu.SemaphoreType.DMA
ZN = 4
YN = 4


def slot_targets(expert_ids, experts_all, capacity):
    rows_local, picks = expert_ids.shape
    flat_ids = expert_ids.reshape(rows_local * picks)
    expert_range = jnp.arange(experts_all, dtype=jnp.int32)
    onehot = (flat_ids[:, None] == expert_range[None, :]).astype(jnp.int32)
    earlier = jnp.cumsum(onehot, axis=0) - onehot
    slot_index = jnp.sum(earlier * onehot, axis=1)
    return (flat_ids * capacity + slot_index).reshape(rows_local, picks)


def push(src, dst, ssem, rsem, axis, target):
    return pltpu.make_async_remote_copy(
        src_ref=src,
        dst_ref=dst,
        send_sem=ssem,
        recv_sem=rsem,
        device_id={axis: target},
        device_id_type=MESH,
    )


def greet(peers):
    barrier = pltpu.get_barrier_semaphore()
    total = 0
    for axis, targets in peers:
        if callable(targets):
            count, of = targets()

            def one(j, carry):
                pl.semaphore_signal(barrier, inc=1, device_id={axis: of(j)}, device_id_type=MESH)
                return carry

            lax.fori_loop(1, count, one, 0)
            total += count - 1
        else:
            for target in targets:
                pl.semaphore_signal(barrier, inc=1, device_id={axis: target}, device_id_type=MESH)
                total += 1
    pl.semaphore_wait(barrier, total)


def everyone(axis):
    def make():
        n = lax.axis_size(axis)
        me = lax.axis_index(axis)
        return n, lambda j: lax.rem(me + j, n)

    return make


def ring_places():
    s = lax.axis_index("seq")
    y, z = lax.div(s, ZN), lax.rem(s, ZN)
    up = lax.rem(y + 1, YN) * ZN + z
    down = lax.rem(y + YN - 1, YN) * ZN + z
    zpeers = [y * ZN + lax.rem(z + k, ZN) for k in range(1, ZN)]
    return s, y, z, up, down, zpeers


GATHER_SEMS = [DMA((ZN,))] * 10


def gather_steps(src, view, sems):
    zs, zr, us, ur, ds, dr, fus, fur, fds, fdr = sems
    s, y, z, up, down, zpeers = ring_places()
    low_y = lax.rem(y + YN - 1, YN)
    high_y = lax.rem(y + 1, YN)

    def column(k):
        return lax.rem(z + ZN - k, ZN)

    def zcopy(k):
        return push(src, view(s, None), zs.at[k], zr.at[k], "seq", zpeers[k - 1])

    def ycopies(k):
        shard = y * ZN + column(k)
        source = src if k == 0 else view(shard, None)
        return (
            push(source, view(shard, None), us.at[k], ur.at[k], "seq", up),
            push(source, view(shard, None), ds.at[k], dr.at[k], "seq", down),
        )

    def forwards(k):
        from_low = view(low_y * ZN + column(k), 0)
        from_high = view(high_y * ZN + column(k), 1)
        return (
            push(from_low, from_low, fus.at[k], fur.at[k], "seq", up),
            push(from_high, from_high, fds.at[k], fdr.at[k], "seq", down),
        )

    def pass_on(k):
        go_up, go_down = ycopies(k)
        first, second = forwards(k)
        go_up.wait_recv()
        first.start()
        go_down.wait_recv()
        second.start()

    def begin():
        for k in range(1, ZN):
            zcopy(k).start()
        for copy in ycopies(0):
            copy.start()

    def rest():
        for k in range(1, ZN):
            zcopy(k).wait_recv()
            for copy in ycopies(k):
                copy.start()
            pass_on(k - 1)
        pass_on(ZN - 1)

    def finish():
        for k in range(ZN):
            for copy in forwards(k):
                copy.wait()
            for copy in ycopies(k):
                copy.wait_send()
        for k in range(1, ZN):
            zcopy(k).wait_send()

    return begin, rest, finish


def swap_steps(axis, pieces, send, recv):
    n = lax.axis_size(axis)
    me = lax.axis_index(axis)

    def copy(i, j):
        target = lax.rem(me + j, n)
        source, landing = pieces[i]
        return push(source(target), landing(me), send.at[i, j], recv.at[i, j], axis, target)

    def begin():
        def one(j, carry):
            for i in range(len(pieces)):
                copy(i, j).start()
            return carry

        lax.fori_loop(1, n, one, 0)

    def finish():
        def one(j, carry):
            for i in range(len(pieces)):
                copy(i, j).wait()
            return carry

        lax.fori_loop(1, n, one, 0)

    return begin, finish


def dispatch_kernel(pack, outgoing, whole, arrived, send, recv, own_sem, *gsems):
    s, y, z, up, down, zpeers = ring_places()
    me = lax.axis_index("lang")

    def view(shard, half):
        columns = pl.ds(pl.multiple_of(shard * HD, HD), HD)
        if half is None:
            return whole.at[:, columns]
        rows = pack.shape[0] // 2
        return whole.at[pl.ds(half * rows, rows), columns]

    gbegin, grest, gfinish = gather_steps(pack, view, gsems)
    sbegin, sfinish = swap_steps(
        "lang", [(lambda t: outgoing.at[t], lambda m: arrived.at[m])], send, recv
    )
    own = [
        pltpu.make_async_copy(pack, view(s, None), own_sem.at[0]),
        pltpu.make_async_copy(outgoing.at[me], arrived.at[me], own_sem.at[1]),
    ]
    greet([("lang", everyone("lang")), ("seq", zpeers + [up, down])])
    sbegin()
    gbegin()
    for copy in own:
        copy.start()
    grest()
    sfinish()
    gfinish()
    for copy in own:
        copy.wait()


def return_kernel(results, returned, send, recv, own_sem):
    me = lax.axis_index("lang")
    begin, finish = swap_steps(
        "lang", [(lambda t: results.at[t], lambda m: returned.at[m])], send, recv
    )
    own = pltpu.make_async_copy(results.at[me], returned.at[me], own_sem.at[0])
    greet([("lang", everyone("lang"))])
    begin()
    own.start()
    finish()
    own.wait()


def prompt_kernel(mixed, q, k, v, g, rows, qh, kh, vh, gh, send, recv, own_sem, *gsems):
    s = lax.axis_index("seq")
    part = q.shape[1]
    count = mixed.shape[0]

    def view(shard, half):
        if half is None:
            return rows.at[pl.ds(pl.multiple_of(shard * count, count), count), :]
        size = count // 2
        return rows.at[pl.ds(pl.multiple_of(shard * count + half * size, size), size), :]

    def source(array):
        return lambda t: array.at[:, :, pl.ds(pl.multiple_of(t * HD, HD), HD)]

    def landing(array):
        return lambda m: array.at[:, pl.ds(pl.multiple_of(m * part, part), part), :]

    pieces = [(source(a), landing(b)) for a, b in ((q, qh), (k, kh), (v, vh), (g, gh))]
    gbegin, grest, gfinish = gather_steps(mixed, view, gsems)
    sbegin, sfinish = swap_steps("seq", pieces, send, recv)
    own = [pltpu.make_async_copy(mixed, view(s, None), own_sem.at[len(pieces)])]
    for i, (a, b) in enumerate(pieces):
        own.append(pltpu.make_async_copy(a(s), b(s), own_sem.at[i]))
    greet([("seq", everyone("seq"))])
    gbegin()
    sbegin()
    for copy in own:
        copy.start()
    grest()
    sfinish()
    gfinish()
    for copy in own:
        copy.wait()


def back_kernel(
    att, qg, kg, vg, partial, att_rows, latent, total, parts, mine, pair, done,
    send, recv, own_sem, rsend, rrecv, psend, precv, asend, arecv,
):
    s = lax.axis_index("seq")
    l = lax.axis_index("lang")
    group = lax.axis_size("lang") // 2
    high, j = lax.div(l, group), lax.rem(l, group)
    part = att_rows.shape[1]
    chunk = partial.shape[0] // group

    def source(array):
        return lambda t: array.at[:, pl.ds(pl.multiple_of(t * part, part), part), :]

    def landing(array):
        return lambda m: array.at[:, :, pl.ds(pl.multiple_of(m * HD, HD), HD)]

    pieces = [
        (source(att), landing(att_rows)),
        (source(qg), landing(latent.at[0])),
        (source(kg), landing(latent.at[1])),
        (source(vg), landing(latent.at[2])),
    ]
    sbegin, sfinish = swap_steps("seq", pieces, send, recv)
    own = [
        pltpu.make_async_copy(a(s), b(s), own_sem.at[i]) for i, (a, b) in enumerate(pieces)
    ]
    greet([("seq", everyone("seq")), ("lang", everyone("lang"))])

    def mate(k):
        return high * group + lax.rem(j + k, group)

    def piece(array, t):
        return array.at[pl.ds(pl.multiple_of(t * chunk, chunk), chunk), :]

    def scatter(k):
        t = lax.rem(j + k, group)
        return push(
            piece(partial, t), parts.at[group - k], rsend.at[k], rrecv.at[k], "lang", mate(k)
        )

    def spread(k):
        return push(done, piece(total, j), asend.at[k], arecv.at[k], "lang", mate(k))

    for k in range(1, group):
        scatter(k).start()
    sbegin()
    for copy in own:
        copy.start()
    keep = pltpu.make_async_copy(piece(partial, j), parts.at[0], own_sem.at[len(pieces)])
    keep.start()
    keep.wait()
    for k in range(1, group):
        scatter(k).wait()
    acc = parts[0].astype(F32)
    for k in range(1, group):
        acc = acc + parts[k].astype(F32)
    mine[...] = acc.astype(BF)
    other = lax.rem(l + group, 2 * group)
    cross = push(mine, pair, psend.at[0], precv.at[0], "lang", other)
    cross.start()
    cross.wait()
    done[...] = (mine[...].astype(F32) + pair[...].astype(F32)).astype(BF)
    for k in range(1, group):
        spread(k).start()
    last = pltpu.make_async_copy(done, piece(total, j), own_sem.at[len(pieces)])
    last.start()
    sfinish()
    for copy in own:
        copy.wait()
    last.wait()
    for k in range(1, group):
        spread(k).wait_send()
        t = lax.rem(j + group - k, group)
        push(done, piece(total, t), asend.at[k], arecv.at[k], "lang", mate(k)).wait_recv()


def attention_kernel(
    lengths, q_ref, g_ref, kl_ref, vl_ref, kp_ref, vp_ref,
    att_ref, qg_ref, kg_ref, vg_ref, pg_ref,
    kt, vt, kacc, vacc, e_s, d_s,
):
    page, block = pl.program_id(0), pl.program_id(1)
    length = lengths[page]
    lat = kl_ref.shape[1]
    keys_all = 2 * lat
    step = 256
    bq = q_ref.shape[1]
    scale = 1.0 / math.sqrt(HD)
    to_two = scale * math.log2(math.e)

    def key_part(i):
        at = i * step
        return kl_ref[0, pl.ds(at, step), :] if at < lat else kp_ref[pl.ds(at - lat, step), :]

    def value_part(i):
        at = i * step
        return vl_ref[0, pl.ds(at, step), :] if at < lat else vp_ref[pl.ds(at - lat, step), :]

    steps = keys_all // step

    @pl.when(block == 0)
    def _():
        for i in range(steps):
            kt[:, pl.ds(i * step, step)] = key_part(i).T
            vt[:, pl.ds(i * step, step)] = value_part(i).T
        kacc[...] = jnp.zeros_like(kacc)
        vacc[...] = jnp.zeros_like(vacc)

    q, g = q_ref[0], g_ref[0]
    nt = (((1,), (1,)), ((), ()))
    highest = jnp.full((1, bq), -jnp.inf, F32)
    for i in range(steps):
        scores = lax.dot_general(key_part(i), q, nt, preferred_element_type=F32)
        if i * step >= lat:
            at = i * step - lat + lax.broadcasted_iota(jnp.int32, (step, bq), 0)
            scores = jnp.where(at < length, scores, -jnp.inf)
        highest = jnp.maximum(highest, jnp.max(scores, axis=0, keepdims=True))
        e_s[pl.ds(i * step, step), :] = scores
    top = highest * to_two
    total = jnp.zeros((1, bq), F32)
    weighted = jnp.zeros((1, bq), F32)
    for i in range(steps):
        raised = jnp.exp2(e_s[pl.ds(i * step, step), :] * to_two - top)
        prob_grad = lax.dot_general(value_part(i), g, nt, preferred_element_type=F32)
        total = total + jnp.sum(raised, axis=0, keepdims=True)
        weighted = weighted + jnp.sum(raised * prob_grad, axis=0, keepdims=True)
        e_s[pl.ds(i * step, step), :] = raised
        d_s[pl.ds(i * step, step), :] = prob_grad
    inverse = 1.0 / total
    centre = weighted * inverse
    scaled = inverse * scale
    att_t = jnp.zeros((HD, bq), F32)
    qg_t = jnp.zeros((HD, bq), F32)
    for i in range(steps):
        at = pl.ds(i * step, step)
        raised = e_s[at, :]
        soft_low = (raised * inverse).astype(BF)
        score_grad = (raised * scaled * (d_s[at, :] - centre)).astype(BF)
        att_t = att_t + jnp.dot(vt[:, at], soft_low, preferred_element_type=F32)
        qg_t = qg_t + jnp.dot(kt[:, at], score_grad, preferred_element_type=F32)
        vacc[at, :] += jnp.dot(soft_low, g, preferred_element_type=F32)
        kacc[at, :] += jnp.dot(score_grad, q, preferred_element_type=F32)
    att_ref[0] = att_t.T.astype(BF)
    qg_ref[0] = qg_t.T.astype(BF)

    @pl.when(block == pl.num_programs(1) - 1)
    def _():
        kg_ref[0] = kacc[pl.ds(0, lat), :].astype(BF)
        vg_ref[0] = vacc[pl.ds(0, lat), :].astype(BF)
        pg_ref[:, pl.ds(0, HD)] = kacc[pl.ds(lat, lat), :].astype(BF)
        pg_ref[:, pl.ds(HD, HD)] = vacc[pl.ds(lat, lat), :].astype(BF)


def attention(lengths, q, g, k, v, kv):
    pages, lat, _ = q.shape
    bq = 256
    row = pl.BlockSpec((1, bq, HD), lambda p, b, _: (p, b, 0))
    full = pl.BlockSpec((1, lat, HD), lambda p, b, _: (p, 0, 0))
    key = pl.BlockSpec((lat, HD), lambda p, b, _: (p, 0))
    value = pl.BlockSpec((lat, HD), lambda p, b, _: (p, 1))
    both = pl.BlockSpec((lat, 2 * HD), lambda p, b, _: (p, 0))
    shape = jax.ShapeDtypeStruct((pages, lat, HD), BF)
    return pl.pallas_call(
        attention_kernel,
        grid_spec=pltpu.PrefetchScalarGridSpec(
            num_scalar_prefetch=1,
            grid=(pages, lat // bq),
            in_specs=[row, row, full, full, key, value],
            out_specs=[row, row, full, full, both],
            scratch_shapes=[
                pltpu.VMEM((HD, 2 * lat), BF),
                pltpu.VMEM((HD, 2 * lat), BF),
                pltpu.VMEM((2 * lat, HD), F32),
                pltpu.VMEM((2 * lat, HD), F32),
                pltpu.VMEM((2 * lat, bq), F32),
                pltpu.VMEM((2 * lat, bq), F32),
            ],
        ),
        out_shape=[shape] * 4 + [jax.ShapeDtypeStruct((pages * lat, 2 * HD), BF)],
        compiler_params=pltpu.CompilerParams(vmem_limit_bytes=48 << 20),
    )(lengths, q, g, k, v, kv, kv)


def remote(body, number, out_shape, scratch, *operands, vmem_outs=()):
    return pl.pallas_call(
        body,
        out_shape=out_shape,
        in_specs=[ANY] * len(operands),
        out_specs=[ANY] * len(out_shape),
        scratch_shapes=scratch,
        compiler_params=pltpu.CompilerParams(
            collective_id=number, has_side_effects=True, vmem_limit_bytes=32 << 20
        ),
    )(*operands)


def local(
    prompt_rows,
    expert_ids,
    expert_gates,
    w_gate,
    w_up,
    w_down,
    w_kv,
    prompt_lengths,
    latent_q,
    latent_k,
    latent_v,
    grad_out,
):
    lang_count = lax.axis_size("lang")
    seq_count = lax.axis_size("seq")
    experts_all = lang_count
    rows_local, model_width = prompt_rows.shape
    ff = w_gate.shape[2]
    capacity = 3 * rows_local // experts_all
    sds = jax.ShapeDtypeStruct
    targets = slot_targets(expert_ids, experts_all, capacity)
    slot_ids = jnp.arange(experts_all * capacity, dtype=jnp.int32)
    dispatch_mask = jnp.any(slot_ids[:, None, None] == targets[None, :, :], axis=2).astype(BF)
    outgoing = jnp.dot(dispatch_mask, prompt_rows, preferred_element_type=F32).astype(BF)
    outgoing = outgoing.reshape(experts_all, capacity, model_width)
    pack = jnp.concatenate([w_gate[0].T, w_up[0].T, w_down[0]], axis=0)
    whole, arrived = remote(
        dispatch_kernel,
        1,
        [sds((3 * ff, model_width), BF), sds(outgoing.shape, BF)],
        [DMA((1, lang_count)), DMA((1, lang_count)), DMA((2,))] + GATHER_SEMS,
        pack,
        outgoing,
    )
    tokens = arrived.reshape(experts_all * capacity, model_width)
    nt = (((1,), (1,)), ((), ()))
    gate_up = lax.dot_general(tokens, whole[: 2 * ff], nt, preferred_element_type=F32)
    hidden = (jax.nn.silu(gate_up[:, :ff]) * gate_up[:, ff:]).astype(BF)
    results = jnp.dot(hidden, whole[2 * ff :], preferred_element_type=F32).astype(BF)
    (returned,) = remote(
        return_kernel,
        2,
        [sds(outgoing.shape, BF)],
        [DMA((1, lang_count)), DMA((1, lang_count)), DMA((1,))],
        results.reshape(outgoing.shape),
    )
    returned = returned.reshape(experts_all * capacity, model_width)
    mixed_sum = jnp.zeros((rows_local, model_width), F32)
    for which in range(targets.shape[1]):
        picker = (targets[:, which][:, None] == slot_ids[None, :]).astype(BF)
        picked = jnp.dot(picker, returned, preferred_element_type=F32)
        mixed_sum = mixed_sum + expert_gates[:, which][:, None] * picked
    mixed = mixed_sum.astype(BF)
    pages, part, _ = latent_q.shape
    lat = part * seq_count
    heads = sds((pages, lat, HD), BF)
    group_rows, qh, kh, vh, gh = remote(
        prompt_kernel,
        3,
        [sds((rows_local * seq_count, model_width), BF)] + [heads] * 4,
        [DMA((4, seq_count)), DMA((4, seq_count)), DMA((5,))] + GATHER_SEMS,
        mixed,
        latent_q,
        latent_k,
        latent_v,
        grad_out,
    )
    kv = jnp.dot(
        group_rows, w_kv.reshape(model_width, 2 * HD), preferred_element_type=F32
    ).astype(BF)
    att, qg, kg, vg, prompt_grad = attention(prompt_lengths, qh, gh, kh, vh, kv)
    partial = lax.dot_general(
        group_rows, prompt_grad, (((0,), (0,)), ((), ())), preferred_element_type=F32
    ).astype(BF)
    half = lang_count // 2
    chunk = model_width // half
    att_rows, latent, total = remote(
        back_kernel,
        4,
        [
            sds(latent_q.shape, BF),
            sds((3,) + latent_q.shape, BF),
            sds(partial.shape, BF),
        ],
        [
            pltpu.VMEM((half, chunk, 2 * HD), BF),
            pltpu.VMEM((chunk, 2 * HD), BF),
            pltpu.VMEM((chunk, 2 * HD), BF),
            pltpu.VMEM((chunk, 2 * HD), BF),
            DMA((4, seq_count)),
            DMA((4, seq_count)),
            DMA((5,)),
            DMA((half,)),
            DMA((half,)),
            DMA((1,)),
            DMA((1,)),
            DMA((half,)),
            DMA((half,)),
        ],
        att,
        qg,
        kg,
        vg,
        partial,
    )
    grad_wkv = total.astype(F32).reshape(model_width, 2, HD)
    return (att_rows, latent, grad_wkv)


def solution(mesh):
    return jax.shard_map(
        local,
        mesh=mesh,
        in_specs=(
            P(("lang", "seq"), None),
            P(("lang", "seq"), None),
            P(("lang", "seq"), None),
            P("lang", "seq", None),
            P("lang", "seq", None),
            P("lang", None, "seq"),
            P(None, None, "seq"),
            P("lang"),
            P("lang", "seq", None),
            P("lang", "seq", None),
            P("lang", "seq", None),
            P("lang", "seq", None),
        ),
        out_specs=(P("lang", "seq", None), P(None, "lang", "seq", None), P(None, None, "seq")),
        check_vma=False,
    )
```

time: 1100 us -> 396 us (0.36); the launches traced: 1070 us -> 396 us
  waiting for transfers between devices: 653 us -> 0 us
  Pallas kernels: 0 us -> 372 us
  local copies, waits for them, and re-layouts: 168 us -> 9.03 us
  starting transfers between devices: 77.8 us -> 0 us
  blocking collectives: 67.4 us -> 0 us
  matrix products: 68.5 us -> 11.7 us
  other arithmetic: 24.4 us -> 2.61 us
  between operations: 14.6 us -> 0.82 us
    pallas_call x0 -> x5, Pallas kernels: none -> 372 us  [the longest x4 351 us: remote(): pl.pallas_call(body, out_shape=out_shape, in_specs=[ANY] * len(operands),...]
    all_gather x4 -> x0, waiting for transfers between devices: 300 us -> none  [the longest x1 93.7 us: local(): lax.all_gather(w_down, 'seq', axis=2, tiled=True)]
    all_to_all x9 -> x0, waiting for transfers between devices: 179 us -> none  [the longest x1 28.5 us: to_heads(): lax.all_to_all(grad_out, 'seq', split_axis=2, concat_axis=1, tiled=True)]
    psum x1 -> x0, waiting for transfers between devices: 172 us -> none  [local(): lax.psum(partial_grad.astype(jnp.bfloat16), 'lang').astype(jnp.float32)]
    dynamic_update_slice x6 -> x0, local copies, waits for them, and re-layouts: 102 us -> none  [local(): lax.map(one_item, (split_heads(query_heads), split_heads(key_heads), spli...]
    all_to_all x9 -> x0, starting transfers between devices: 77.6 us -> none  [the longest x1 22.2 us: to_heads(): lax.all_to_all(latent_q, 'seq', split_axis=2, concat_axis=1, tiled=True)]
    all_to_all x1 -> x0, blocking collectives: 67.4 us -> none  [local(): lax.all_to_all(outgoing, 'lang', split_axis=0, concat_axis=1, tiled=True)]
    dot_general x30 -> x6, matrix products: 61.8 us -> 9.07 us  [the longest x1 3.43 us: local(): jnp.dot(group_rows, w_kv.reshape(model_width, 2 * HD), preferred_element_...]
  transfers between devices with their start and end apart: 14 -> 0, of which waited for: 14 -> 0; matrix products, arithmetic and copies ran while one was open for 4% -> 0% of each run, Pallas kernels for 0% -> 0%
where the time goes in v1:
time: 396 us
  Pallas kernels  372 us (94%)
  matrix products  11.7 us (3%)
  local copies, waits for them, and re-layouts  9.03 us (2%)
    pallas_call x4, Pallas kernels, remote(): pl.pallas_call(body, out_shape=out_shape, in_specs=[ANY] * len(operands),...  351 us
    pallas_call x1, Pallas kernels, attention(): pl.pallas_call(attention_kernel, grid_spec=pltpu.PrefetchScalarGridSpec(n...  21.3 us

profile of v1, /device:TPU:1, one launch (start us, length us, event | category | flops | bytes accessed | tf_op | source)
XLA Modules:
  0.0 396.1 jit_solution(2233830646922647220)
XLA Ops:
  0.6 0.8 slice_bitcast_fusion.1
  1.4 0.8 copy.32
  2.5 0.6 reduce-window.6
  3.1 0.2 slice_reduce_fusion
  3.6 0.7 multiply_add_fusion
  4.4 1.1 pad_maximum_fusion.pack
  5.5 0.6 convolution_convert_fusion
  6.1 125.9 %shard_map.139 = (bf16[2112,2048]{1,0:T(8,128)(2,1)S(1)}, bf16[16,24,2048]{2,1,0:T(8,128)(2,1)S(1)}) custom-call(bf16[2112,128]{1,0:T(8,128)(2,1)S(1)} %pad_maximum_fusion.pack, bf16[16,24,2048]{2,1,0:T(8,128)(2,1)S(1)} %bitcast.52), custom_call_target="tpu_custom_call" | custom-call | tf_op jit(solution)/shard_map/pallas_call | solution.py:437
  132.0 2.6 fusion
  134.6 1.5 fusion.4
  136.1 39.2 %shard_map.140 = bf16[16,24,2048]{2,1,0:T(8,128)(2,1)S(1)} custom-call(bf16[16,24,2048]{2,1,0:T(8,128)(2,1)S(1)} %bitcast.53), custom_call_target="tpu_custom_call" | custom-call | tf_op jit(solution)/shard_map/pallas_call | solution.py:437
  175.2 0.5 convolution_multiply_fusion.1
  175.8 0.5 fusion.8.mixed
  176.3 0.5 copy-done.1
  176.9 0.2 copy-done.3
  177.3 97.1 %shard_map.141 = (bf16[2048,2048]{1,0:T(8,128)(2,1)S(1)}, bf16[2,1024,128]{2,1,0:T(8,128)(2,1)S(1)}, bf16[2,1024,128]{2,1,0:T(8,128)(2,1)S(1)}, bf16[2,1024,128]...) custom-call(bf16[128,2048]{1,0:T(8,128)(2,1)S(1)} %fusion.8.mixed, bf16[2,64,2048]{2,1,0:T(8,128)(2,1)S(1)} %copy-done.1, ...), custom_call_target="tpu_custom_call" | custom-call | tf_op jit(solution)/shard_map/pallas_call | solution.py:437
  274.4 3.4 convolution_convert_fusion.2.kp_ref.vp_ref
  277.8 21.3 %shard_map.142 = (bf16[2,1024,128]{2,1,0:T(8,128)(2,1)S(1)}, bf16[2,1024,128]{2,1,0:T(8,128)(2,1)S(1)}, bf16[2,1024,128]{2,1,0:T(8,128)(2,1)S(1)}, bf16[2,1024,1...) custom-call(s32[2]{0:T(128)S(1)} %copy-done.6, bf16[2,1024,128]{2,1,0:T(8,128)(2,1)S(1)} %get-tuple-element.20.q_ref, ...), custom_call_target="tpu_custom_call" | custom-call | tf_op jit(solution)/shard_map/pallas_call | solution.py:415
  299.2 2.7 convolution_convert_fusion.1.partial
  301.8 88.4 %shard_map.143 = (bf16[2,64,2048]{2,1,0:T(8,128)(2,1)S(1)}, bf16[3,2,64,2048]{3,2,1,0:T(8,128)(2,1)S(1)}, bf16[2048,256]{1,0:T(8,128)(2,1)S(1)}) custom-call(bf16[2,1024,128]{2,1,0:T(8,128)(2,1)S(1)} %get-tuple-element.25.att, bf16[2,1024,128]{2,1,0:T(8,128)(2,1)S(1)} %get-tuple-element.26.qg, bf16[2,1024,128]{2,1,0:T(8,128)(2,1)S(1)} %get-tuple-element.27.kg, ...), custom_call_target="tpu_custom_call" | custom-call | tf_op jit(solution)/shard_map/pallas_call | solution.py:437
  390.3 0.8 copy-done.5
  391.1 2.0 reshape.62
  393.1 1.9 copy.45
  394.9 1.1 copy.46
  (23 shorter events, 1.0 us)
Async XLA Ops:
  0.6 4.9 %copy-start = (bf16[128,2048]{1,0:T(8,128)(2,1)S(1)}, bf16[128,2048]{1,0:T(8,128)(2,1)}, u32[]{:S(2)}) copy-start(bf16[128,2048]{1,0:T(8,128)(2,1)} %param.12) | copy-start | bytes 1572868
  175.7 1.0 copy-start.1
  175.7 1.2 copy-start.2
  175.8 1.3 copy-start.3
  175.8 1.5 copy-start.4
  177.3 97.1 %copy-start.7 = (bf16[2048,2,128]{2,1,0:T(2,128)(2,1)S(1)}, bf16[2048,2,128]{2,1,0:T(2,128)(2,1)}, u32[]{:S(2)}) copy-start(bf16[2048,2,128]{2,1,0:T(2,128)(2,1)} %param.18) | copy-start | bytes 3145732
  274.4 3.4 copy-start.6
  390.3 0.8 copy-start.5

commit v2 on v1

--- a/solution.py
+++ b/solution.py
@@ -1,4 +1,3 @@
-import functools
 import math
 
 import jax
@@ -15,6 +14,7 @@
 F32 = jnp.float32
 DMA = pltpu.SemaphoreType.DMA
 ZN = 4
+CHUNKS = 2
 YN = 4
 
 
@@ -39,24 +39,23 @@
     )
 
 
-def greet(peers):
+def greet(axes):
+    pl.semaphore_wait(pltpu.get_barrier_semaphore(), greet_all(axes))
+
+
+def greet_all(axes):
     barrier = pltpu.get_barrier_semaphore()
     total = 0
-    for axis, targets in peers:
-        if callable(targets):
-            count, of = targets()
-
-            def one(j, carry):
-                pl.semaphore_signal(barrier, inc=1, device_id={axis: of(j)}, device_id_type=MESH)
-                return carry
-
-            lax.fori_loop(1, count, one, 0)
-            total += count - 1
-        else:
-            for target in targets:
-                pl.semaphore_signal(barrier, inc=1, device_id={axis: target}, device_id_type=MESH)
-                total += 1
-    pl.semaphore_wait(barrier, total)
+    for axis in axes:
+        count, of = everyone(axis)()
+
+        def one(j, carry):
+            pl.semaphore_signal(barrier, inc=1, device_id={axis: of(j)}, device_id_type=MESH)
+            return carry
+
+        lax.fori_loop(1, count, one, 0)
+        total += count - 1
+    return total
 
 
 def everyone(axis):
@@ -73,73 +72,109 @@
     y, z = lax.div(s, ZN), lax.rem(s, ZN)
     up = lax.rem(y + 1, YN) * ZN + z
     down = lax.rem(y + YN - 1, YN) * ZN + z
-    zpeers = [y * ZN + lax.rem(z + k, ZN) for k in range(1, ZN)]
-    return s, y, z, up, down, zpeers
-
-
-GATHER_SEMS = [DMA((ZN,))] * 10
-
-
-def gather_steps(src, view, sems):
-    zs, zr, us, ur, ds, dr, fus, fur, fds, fdr = sems
-    s, y, z, up, down, zpeers = ring_places()
+    return s, y, z, up, down
+
+
+def gather_sems(chunks):
+    return [DMA((chunks, ZN))] * 11
+
+
+def gather_steps(source, view, sems):
+    zl, zr, zin, us, ur, ds, dr, fus, fur, fds, fdr = sems
+    s, y, z, up, down = ring_places()
     low_y = lax.rem(y + YN - 1, YN)
     high_y = lax.rem(y + 1, YN)
 
-    def column(k):
-        return lax.rem(z + ZN - k, ZN)
-
-    def zcopy(k):
-        return push(src, view(s, None), zs.at[k], zr.at[k], "seq", zpeers[k - 1])
-
-    def ycopies(k):
-        shard = y * ZN + column(k)
-        source = src if k == 0 else view(shard, None)
+    def along(c, col, to_right, own):
+        shard = y * ZN + col
+        return push(
+            source(c) if own else view(c, shard, None),
+            view(c, shard, None),
+            (zr if to_right else zl).at[c, col],
+            zin.at[c, col],
+            "seq",
+            s + 1 if to_right else s - 1,
+        )
+
+    def across(c, col, own):
+        shard = y * ZN + col
+        src = source(c) if own else view(c, shard, None)
+        dst = view(c, shard, None)
         return (
-            push(source, view(shard, None), us.at[k], ur.at[k], "seq", up),
-            push(source, view(shard, None), ds.at[k], dr.at[k], "seq", down),
+            push(src, dst, us.at[c, col], ur.at[c, col], "seq", up),
+            push(src, dst, ds.at[c, col], dr.at[c, col], "seq", down),
         )
 
-    def forwards(k):
-        from_low = view(low_y * ZN + column(k), 0)
-        from_high = view(high_y * ZN + column(k), 1)
+    def forwards(c, col):
+        low = view(c, low_y * ZN + col, 0)
+        high = view(c, high_y * ZN + col, 1)
         return (
-            push(from_low, from_low, fus.at[k], fur.at[k], "seq", up),
-            push(from_high, from_high, fds.at[k], fdr.at[k], "seq", down),
+            push(low, low, fus.at[c, col], fur.at[c, col], "seq", up),
+            push(high, high, fds.at[c, col], fdr.at[c, col], "seq", down),
         )
 
-    def pass_on(k):
-        go_up, go_down = ycopies(k)
-        first, second = forwards(k)
+    def pass_on(c, col):
+        go_up, go_down = across(c, col, False)
+        first, second = forwards(c, col)
         go_up.wait_recv()
         first.start()
         go_down.wait_recv()
         second.start()
 
-    def begin():
-        for k in range(1, ZN):
-            zcopy(k).start()
-        for copy in ycopies(0):
+    def each_side(t, do):
+        @pl.when(z >= t)
+        def _():
+            do(z - t, True)
+
+        @pl.when(z + t <= ZN - 1)
+        def _():
+            do(z + t, False)
+
+    def on_way(to_right, do):
+        @pl.when(z < ZN - 1 if to_right else z > 0)
+        def _():
+            do()
+
+    def begin(c):
+        for to_right in (True, False):
+            on_way(to_right, lambda: along(c, z, to_right, True).start())
+        for copy in across(c, z, True):
             copy.start()
 
-    def rest():
-        for k in range(1, ZN):
-            zcopy(k).wait_recv()
-            for copy in ycopies(k):
+    def step(c, t):
+        def arrive(col, to_right):
+            along(c, col, to_right, False).wait_recv()
+            on_way(to_right, lambda: along(c, col, to_right, False).start())
+            for copy in across(c, col, False):
                 copy.start()
-            pass_on(k - 1)
-        pass_on(ZN - 1)
-
-    def finish():
-        for k in range(ZN):
-            for copy in forwards(k):
-                copy.wait()
-            for copy in ycopies(k):
-                copy.wait_send()
-        for k in range(1, ZN):
-            zcopy(k).wait_send()
-
-    return begin, rest, finish
+
+        each_side(t, arrive)
+
+    def relay(c, t):
+        if t == 0:
+            pass_on(c, z)
+        else:
+            each_side(t, lambda col, to_right: pass_on(c, col))
+
+    def finish(c):
+        for to_right in (True, False):
+            on_way(to_right, lambda: along(c, z, to_right, True).wait_send())
+        for copy in across(c, z, True):
+            copy.wait_send()
+        for copy in forwards(c, z):
+            copy.wait()
+        for t in range(1, ZN):
+
+            def ended(col, to_right):
+                on_way(to_right, lambda: along(c, col, to_right, False).wait_send())
+                for copy in across(c, col, False):
+                    copy.wait_send()
+                for copy in forwards(c, col):
+                    copy.wait()
+
+            each_side(t, ended)
+
+    return begin, step, relay, finish
 
 
 def swap_steps(axis, pieces, send, recv):
@@ -170,82 +205,159 @@
     return begin, finish
 
 
-def dispatch_kernel(pack, outgoing, whole, arrived, send, recv, own_sem, *gsems):
-    s, y, z, up, down, zpeers = ring_places()
+def latent_pieces(pairs):
+    part = pairs[0][0].shape[1]
+
+    def source(array):
+        return lambda t: array.at[:, :, pl.ds(pl.multiple_of(t * HD, HD), HD)]
+
+    def landing(array):
+        return lambda m: array.at[:, pl.ds(pl.multiple_of(m * part, part), part), :]
+
+    return [(source(a), landing(b)) for a, b in pairs]
+
+
+def dispatch_kernel(
+    pack, outgoing, q, g, whole, arrived, qh, gh, send, recv, lsend, lrecv, own_sem, *gsems
+):
+    s = lax.axis_index("seq")
+    pieces = latent_pieces([(q, qh), (g, gh)])
+    lbegin, lfinish = swap_steps("seq", pieces, lsend, lrecv)
     me = lax.axis_index("lang")
-
-    def view(shard, half):
+    chunks = 3
+    size = pack.shape[0] // chunks
+
+    def view(c, shard, half):
         columns = pl.ds(pl.multiple_of(shard * HD, HD), HD)
         if half is None:
-            return whole.at[:, columns]
-        rows = pack.shape[0] // 2
-        return whole.at[pl.ds(half * rows, rows), columns]
-
-    gbegin, grest, gfinish = gather_steps(pack, view, gsems)
+            return whole.at[pl.ds(c * size, size), columns]
+        rows = size // 2
+        return whole.at[pl.ds(c * size + half * rows, rows), columns]
+
+    begin, step, relay, finish = gather_steps(
+        lambda c: pack.at[pl.ds(c * size, size), :], view, gsems
+    )
     sbegin, sfinish = swap_steps(
         "lang", [(lambda t: outgoing.at[t], lambda m: arrived.at[m])], send, recv
     )
     own = [
-        pltpu.make_async_copy(pack, view(s, None), own_sem.at[0]),
+        pltpu.make_async_copy(
+            pack, whole.at[:, pl.ds(pl.multiple_of(s * HD, HD), HD)], own_sem.at[0]
+        ),
         pltpu.make_async_copy(outgoing.at[me], arrived.at[me], own_sem.at[1]),
     ]
-    greet([("lang", everyone("lang")), ("seq", zpeers + [up, down])])
-    sbegin()
-    gbegin()
-    for copy in own:
-        copy.start()
-    grest()
-    sfinish()
-    gfinish()
-    for copy in own:
-        copy.wait()
-
-
-def return_kernel(results, returned, send, recv, own_sem):
-    me = lax.axis_index("lang")
-    begin, finish = swap_steps(
-        "lang", [(lambda t: results.at[t], lambda m: returned.at[m])], send, recv
-    )
-    own = pltpu.make_async_copy(results.at[me], returned.at[me], own_sem.at[0])
-    greet([("lang", everyone("lang"))])
-    begin()
-    own.start()
-    finish()
-    own.wait()
-
-
-def prompt_kernel(mixed, q, k, v, g, rows, qh, kh, vh, gh, send, recv, own_sem, *gsems):
-    s = lax.axis_index("seq")
-    part = q.shape[1]
-    count = mixed.shape[0]
-
-    def view(shard, half):
-        if half is None:
-            return rows.at[pl.ds(pl.multiple_of(shard * count, count), count), :]
-        size = count // 2
-        return rows.at[pl.ds(pl.multiple_of(shard * count + half * size, size), size), :]
-
-    def source(array):
-        return lambda t: array.at[:, :, pl.ds(pl.multiple_of(t * HD, HD), HD)]
-
-    def landing(array):
-        return lambda m: array.at[:, pl.ds(pl.multiple_of(m * part, part), part), :]
-
-    pieces = [(source(a), landing(b)) for a, b in ((q, qh), (k, kh), (v, vh), (g, gh))]
-    gbegin, grest, gfinish = gather_steps(mixed, view, gsems)
-    sbegin, sfinish = swap_steps("seq", pieces, send, recv)
-    own = [pltpu.make_async_copy(mixed, view(s, None), own_sem.at[len(pieces)])]
     for i, (a, b) in enumerate(pieces):
-        own.append(pltpu.make_async_copy(a(s), b(s), own_sem.at[i]))
-    greet([("seq", everyone("seq"))])
-    gbegin()
+        own.append(pltpu.make_async_copy(a(s), b(s), own_sem.at[i + 2]))
+    greet(["lang", "seq"])
+    for c in range(chunks):
+        begin(c)
     sbegin()
     for copy in own:
         copy.start()
-    grest()
+    for t in range(1, ZN):
+        for c in range(chunks):
+            step(c, t)
+            relay(c, t - 1)
+        if t == 1:
+            lbegin()
+    for c in range(chunks):
+        relay(c, ZN - 1)
     sfinish()
-    gfinish()
+    lfinish()
+    for c in range(chunks):
+        finish(c)
     for copy in own:
+        copy.wait()
+
+
+def prompt_kernel(
+    results, pick, gates, k, v, rows, kh, vh,
+    returned, mixed, rsend, rrecv, send, recv, own_sem, *gsems,
+):
+    s = lax.axis_index("seq")
+    me = lax.axis_index("lang")
+    count, width = mixed.shape
+    chunks = rsend.shape[0]
+    wide = width // chunks
+
+    def view(c, shard, half):
+        columns = pl.ds(c * wide, wide)
+        if half is None:
+            return rows.at[pl.ds(pl.multiple_of(shard * count, count), count), columns]
+        size = count // 2
+        at = pl.multiple_of(shard * count + half * size, size)
+        return rows.at[pl.ds(at, size), columns]
+
+    pieces = latent_pieces([(k, kh), (v, vh)])
+    begin, step, relay, finish = gather_steps(
+        lambda c: mixed.at[:, pl.ds(c * wide, wide)], view, gsems
+    )
+    swaps = [
+        swap_steps("seq", [pieces[i]], send.at[pl.ds(i, 1)], recv.at[pl.ds(i, 1)])
+        for i in range(2)
+    ]
+
+    def back(c):
+        columns = pl.ds(c * wide, wide)
+        return swap_steps(
+            "lang",
+            [(lambda t: results.at[t, :, columns], lambda m: returned.at[m, :, columns])],
+            rsend.at[pl.ds(c, 1)],
+            rrecv.at[pl.ds(c, 1)],
+        )
+
+    backs = [back(c) for c in range(chunks)]
+    own = [pltpu.make_async_copy(results.at[me], returned.at[me], own_sem.at[0])]
+    for i, (a, b) in enumerate(pieces):
+        own.append(pltpu.make_async_copy(a(s), b(s), own_sem.at[i + 1]))
+    greet(["seq", "lang"])
+    for copy in own:
+        copy.start()
+    for c in range(chunks):
+        backs[c][0]()
+    own[0].wait()
+    places = []
+
+    def mix(c):
+        backs[c][1]()
+        columns = pl.ds(c * wide, wide)
+        slots = returned[:, :, columns].astype(F32)
+        slots = slots.reshape(slots.shape[0] * slots.shape[1], wide).astype(BF)
+        total = jnp.zeros((count, wide), F32)
+        for which in range(pick.shape[0]):
+            picked = jnp.dot(pick[which], slots, preferred_element_type=F32)
+            total = total + gates[:, which : which + 1] * picked
+        mixed[:, columns] = total.astype(BF)
+        place = pltpu.make_async_copy(
+            mixed.at[:, columns], view(c, s, None), own_sem.at[3 + c]
+        )
+        place.start()
+        places.append(place)
+        begin(c)
+
+    mix(0)
+    swaps[0][0]()
+    step(0, 1)
+    mix(1)
+    relay(0, 0)
+    step(0, 2)
+    step(1, 1)
+    swaps[1][0]()
+    relay(0, 1)
+    relay(1, 0)
+    step(0, 3)
+    step(1, 2)
+    relay(0, 2)
+    relay(1, 1)
+    step(1, 3)
+    relay(0, 3)
+    relay(1, 2)
+    relay(1, 3)
+    for swap in swaps:
+        swap[1]()
+    for c in range(chunks):
+        finish(c)
+    for copy in own[1:] + places:
         copy.wait()
 
 
@@ -276,7 +388,7 @@
     own = [
         pltpu.make_async_copy(a(s), b(s), own_sem.at[i]) for i, (a, b) in enumerate(pieces)
     ]
-    greet([("seq", everyone("seq")), ("lang", everyone("lang"))])
+    greet(["seq", "lang"])
 
     def mate(k):
         return high * group + lax.rem(j + k, group)
@@ -433,11 +545,14 @@
     )(lengths, q, g, k, v, kv, kv)
 
 
-def remote(body, number, out_shape, scratch, *operands, vmem_outs=()):
+def remote(body, number, out_shape, scratch, *operands, in_vmem=()):
     return pl.pallas_call(
         body,
         out_shape=out_shape,
-        in_specs=[ANY] * len(operands),
+        in_specs=[
+            pl.BlockSpec(memory_space=pltpu.VMEM) if i in in_vmem else ANY
+            for i in range(len(operands))
+        ],
         out_specs=[ANY] * len(out_shape),
         scratch_shapes=scratch,
         compiler_params=pltpu.CompilerParams(
@@ -473,46 +588,52 @@
     outgoing = jnp.dot(dispatch_mask, prompt_rows, preferred_element_type=F32).astype(BF)
     outgoing = outgoing.reshape(experts_all, capacity, model_width)
     pack = jnp.concatenate([w_gate[0].T, w_up[0].T, w_down[0]], axis=0)
-    whole, arrived = remote(
+    pages, part, _ = latent_q.shape
+    lat = part * seq_count
+    heads = sds((pages, lat, HD), BF)
+    whole, arrived, qh, gh = remote(
         dispatch_kernel,
         1,
-        [sds((3 * ff, model_width), BF), sds(outgoing.shape, BF)],
-        [DMA((1, lang_count)), DMA((1, lang_count)), DMA((2,))] + GATHER_SEMS,
+        [sds((3 * ff, model_width), BF), sds(outgoing.shape, BF), heads, heads],
+        [
+            DMA((1, lang_count)),
+            DMA((1, lang_count)),
+            DMA((2, seq_count)),
+            DMA((2, seq_count)),
+            DMA((4,)),
+        ]
+        + gather_sems(3),
         pack,
         outgoing,
+        latent_q,
+        grad_out,
     )
     tokens = arrived.reshape(experts_all * capacity, model_width)
     nt = (((1,), (1,)), ((), ()))
     gate_up = lax.dot_general(tokens, whole[: 2 * ff], nt, preferred_element_type=F32)
     hidden = (jax.nn.silu(gate_up[:, :ff]) * gate_up[:, ff:]).astype(BF)
     results = jnp.dot(hidden, whole[2 * ff :], preferred_element_type=F32).astype(BF)
-    (returned,) = remote(
-        return_kernel,
-        2,
-        [sds(outgoing.shape, BF)],
-        [DMA((1, lang_count)), DMA((1, lang_count)), DMA((1,))],
-        results.reshape(outgoing.shape),
-    )
-    returned = returned.reshape(experts_all * capacity, model_width)
-    mixed_sum = jnp.zeros((rows_local, model_width), F32)
-    for which in range(targets.shape[1]):
-        picker = (targets[:, which][:, None] == slot_ids[None, :]).astype(BF)
-        picked = jnp.dot(picker, returned, preferred_element_type=F32)
-        mixed_sum = mixed_sum + expert_gates[:, which][:, None] * picked
-    mixed = mixed_sum.astype(BF)
-    pages, part, _ = latent_q.shape
-    lat = part * seq_count
-    heads = sds((pages, lat, HD), BF)
-    group_rows, qh, kh, vh, gh = remote(
+    pick = (targets.T[:, :, None] == slot_ids[None, None, :]).astype(BF)
+    group_rows, kh, vh = remote(
         prompt_kernel,
         3,
-        [sds((rows_local * seq_count, model_width), BF)] + [heads] * 4,
-        [DMA((4, seq_count)), DMA((4, seq_count)), DMA((5,))] + GATHER_SEMS,
-        mixed,
-        latent_q,
+        [sds((rows_local * seq_count, model_width), BF)] + [heads] * 2,
+        [
+            pltpu.VMEM(outgoing.shape, BF),
+            pltpu.VMEM((rows_local, model_width), BF),
+            DMA((CHUNKS, lang_count)),
+            DMA((CHUNKS, lang_count)),
+            DMA((2, seq_count)),
+            DMA((2, seq_count)),
+            DMA((3 + CHUNKS,)),
+        ]
+        + gather_sems(CHUNKS),
+        results.reshape(outgoing.shape),
+        pick,
+        expert_gates,
         latent_k,
         latent_v,
-        grad_out,
+        in_vmem=(1, 2),
     )
     kv = jnp.dot(
         group_rows, w_kv.reshape(model_width, 2 * HD), preferred_element_type=F32

time: 396 us -> 343 us (0.87)
  Pallas kernels: 372 us -> 319 us
    pallas_call x4 -> x3, Pallas kernels: 351 us -> 298 us  [remote(): pl.pallas_call(body, out_shape=out_shape, in_specs=[pl.BlockSpec(memory_s...]
where the time goes in v2:
time: 343 us; the launch traced here: 341 us
  Pallas kernels  319 us (93%)
  matrix products  10.7 us (3%)
  local copies, waits for them, and re-layouts  8.21 us (2%)
    pallas_call x3, Pallas kernels, remote(): pl.pallas_call(body, out_shape=out_shape, in_specs=[pl.BlockSpec(memory_s...  298 us
    pallas_call x1, Pallas kernels, attention(): pl.pallas_call(attention_kernel, grid_spec=pltpu.PrefetchScalarGridSpec(n...  21.2 us

profile of v2, /device:TPU:1, one launch (start us, length us, event | category | flops | bytes accessed | tf_op | source)
XLA Modules:
  0.0 341.4 jit_solution(6971588282928960598)
XLA Ops:
  0.7 0.9 copy.32
  1.6 0.1 eq.56
  1.7 0.1 eq.52
  1.9 0.6 reduce-window.6
  2.5 0.2 slice_reduce_fusion
  2.7 0.1 fusion.16
  2.8 0.1 reduce_sum.12
  3.0 0.7 multiply_add_fusion
  3.7 0.8 copy.36.gates
  4.5 0.1 fusion.13.pick
  4.6 1.1 pad_maximum_fusion.pack
  5.8 0.6 convolution_convert_fusion
  6.4 116.3 %shard_map.139 = (bf16[2112,2048]{1,0:T(8,128)(2,1)S(1)}, bf16[16,24,2048]{2,1,0:T(8,128)(2,1)S(1)}, bf16[2,1024,128]{2,1,0:T(8,128)(2,1)S(1)}, bf16[2,1024,128]{2,1,0:T(8,128)(2,1)S(1)}) custom-call(bf16[2112,128]{1,0:T(8,128)(2,1)S(1)} %pad_maximum_fusion.pack, bf16[16,24,2048]{2,1,0:T(8,128)(2,1)S(1)} %bitcast.40, bf16[2,64,2048]{2,1,0:T(8,128)(2,1)S(1)} %copy-done.2, ...), custom_call_target="tpu_custom_call" | custom-call | tf_op jit(solution)/shard_map/pallas_call | solution.py:549
  122.7 2.6 fusion
  125.3 1.4 fusion.4
  126.8 116.5 %shard_map.140 = (bf16[2048,2048]{1,0:T(8,128)(2,1)S(1)}, bf16[2,1024,128]{2,1,0:T(8,128)(2,1)S(1)}, bf16[2,1024,128]{2,1,0:T(8,128)(2,1)S(1)}) custom-call(bf16[16,24,2048]{2,1,0:T(8,128)(2,1)S(1)} %bitcast.41, bf16[2,128,384]{2,1,0:T(8,128)(2,1)S(1)} %fusion.13.pick, f32[128,2]{1,0:T(8,128)S(1)} %copy.36.gates, bf16[2,64,2048]{2,1,0:T(8,128)(2,1)S(1)} %copy-done.4, ...), custom_call_target="tpu_custom_call" | custom-call | tf_op jit(solution)/shard_map/pallas_call | solution.py:549
  243.4 3.4 %convolution_convert_fusion.2.kp_ref.vp_ref = bf16[2048,256]{1,0:T(8,128)(2,1)} fusion(bf16[2048,2048]{1,0:T(8,128)(2,1)S(1)} %get-tuple-element.24, bf16[256,8,2,128]{3,2,1,0:T(2,128)(2,1)S(1)} %bitcast.47), kind=kOutput, calls=%fused_computation.7 | convolution fusion | flops 2148007936 | bytes 10485760 | tf_op jit(solution)/shard_map/dot_general | solution.py:638
  246.8 21.2 %shard_map.141 = (bf16[2,1024,128]{2,1,0:T(8,128)(2,1)S(1)}, bf16[2,1024,128]{2,1,0:T(8,128)(2,1)S(1)}, bf16[2,1024,128]{2,1,0:T(8,128)(2,1)S(1)}, bf16[2,1024,1...) custom-call(s32[2]{0:T(128)S(1)} %copy-done.6, bf16[2,1024,128]{2,1,0:T(8,128)(2,1)S(1)} %get-tuple-element.18.q_ref, ...), custom_call_target="tpu_custom_call" | custom-call | tf_op jit(solution)/shard_map/pallas_call | solution.py:527
  268.0 2.7 convolution_convert_fusion.1.partial
  270.6 64.9 %shard_map.142 = (bf16[2,64,2048]{2,1,0:T(8,128)(2,1)S(1)}, bf16[3,2,64,2048]{3,2,1,0:T(8,128)(2,1)S(1)}, bf16[2048,256]{1,0:T(8,128)(2,1)S(1)}) custom-call(bf16[2,1024,128]{2,1,0:T(8,128)(2,1)S(1)} %get-tuple-element.25.att, bf16[2,1024,128]{2,1,0:T(8,128)(2,1)S(1)} %get-tuple-element.26.qg, bf16[2,1024,128]{2,1,0:T(8,128)(2,1)S(1)} %get-tuple-element.27.kg, ...), custom_call_target="tpu_custom_call" | custom-call | tf_op jit(solution)/shard_map/pallas_call | solution.py:549
  335.6 0.8 copy-done.1
  336.4 2.0 reshape.59
  338.4 1.9 copy.46
  340.2 1.1 copy.47
  (20 shorter events, 0.2 us)
Async XLA Ops:
  0.6 5.1 %copy-start = (bf16[128,2048]{1,0:T(8,128)(2,1)S(1)}, bf16[128,2048]{1,0:T(8,128)(2,1)}, u32[]{:S(2)}) copy-start(bf16[128,2048]{1,0:T(8,128)(2,1)} %param.12) | copy-start | bytes 1572868
  0.6 5.7 %copy-start.3 = (bf16[2,64,2048]{2,1,0:T(8,128)(2,1)S(1)}, bf16[2,64,2048]{2,1,0:T(8,128)(2,1)}, u32[]{:S(2)}) copy-start(bf16[2,64,2048]{2,1,0:T(8,128)(2,1)} %g.1) | copy-start | bytes 1572868
  0.7 5.7 %copy-start.2 = (bf16[2,64,2048]{2,1,0:T(8,128)(2,1)S(1)}, bf16[2,64,2048]{2,1,0:T(8,128)(2,1)}, u32[]{:S(2)}) copy-start(bf16[2,64,2048]{2,1,0:T(8,128)(2,1)} %q.1) | copy-start | bytes 1572868
  125.3 1.5 copy-start.4
  125.3 1.5 copy-start.5
  126.8 116.6 %copy-start.7 = (bf16[2048,2,128]{2,1,0:T(2,128)(2,1)S(1)}, bf16[2048,2,128]{2,1,0:T(2,128)(2,1)}, u32[]{:S(2)}) copy-start(bf16[2048,2,128]{2,1,0:T(2,128)(2,1)} %param.18) | copy-start | bytes 3145732
  243.4 3.4 %copy-start.6 = (s32[2]{0:T(128)S(1)}, s32[2]{0:T(128)}, u32[]{:S(2)}) copy-start(s32[2]{0:T(128)} %lengths.1) | copy-start | bytes 28
  335.6 0.8 copy-start.1

commit v3 on v2

--- a/solution.py
+++ b/solution.py
@@ -361,202 +361,224 @@
         copy.wait()
 
 
-def back_kernel(
-    att, qg, kg, vg, partial, att_rows, latent, total, parts, mine, pair, done,
+def attend_kernel(
+    lengths, q_ref, g_ref, k_ref, v_ref, kv_ref, rows_hbm, att_rows, latent, total,
+    rows, att, qg, kg, vg, pg_t, kt, vt, kacc, vacc, e_s, d_s,
+    outbound, parts, mine, pair, done,
     send, recv, own_sem, rsend, rrecv, psend, precv, asend, arecv,
 ):
     s = lax.axis_index("seq")
     l = lax.axis_index("lang")
+    n = lax.axis_size("seq")
+    y = lax.div(s, ZN)
     group = lax.axis_size("lang") // 2
     high, j = lax.div(l, group), lax.rem(l, group)
+    pages, lat, _ = q_ref.shape
     part = att_rows.shape[1]
-    chunk = partial.shape[0] // group
-
-    def source(array):
-        return lambda t: array.at[:, pl.ds(pl.multiple_of(t * part, part), part), :]
-
-    def landing(array):
-        return lambda m: array.at[:, :, pl.ds(pl.multiple_of(m * HD, HD), HD)]
-
-    pieces = [
-        (source(att), landing(att_rows)),
-        (source(qg), landing(latent.at[0])),
-        (source(kg), landing(latent.at[1])),
-        (source(vg), landing(latent.at[2])),
-    ]
-    sbegin, sfinish = swap_steps("seq", pieces, send, recv)
-    own = [
-        pltpu.make_async_copy(a(s), b(s), own_sem.at[i]) for i, (a, b) in enumerate(pieces)
-    ]
+    chunk = rows.shape[1] // group
+    sources = [att, qg, kg, vg]
+    landings = [att_rows, latent.at[0], latent.at[1], latent.at[2]]
+    fetch = pltpu.make_async_copy(rows_hbm, rows, own_sem.at[0])
+    fetch.start()
     greet(["seq", "lang"])
+
+    def out(i, page, to, frm):
+        return push(
+            sources[i].at[page, pl.ds(pl.multiple_of(to * part, part), part), :],
+            landings[i].at[page, :, pl.ds(pl.multiple_of(frm * HD, HD), HD)],
+            send.at[i, page, to],
+            recv.at[i, page, frm],
+            "seq",
+            to,
+        )
+
+    step = 256
+    blocks = YN
+    bq = lat // blocks
+    keys_all = 2 * lat
+    steps = keys_all // step
+    scale = 1.0 / math.sqrt(HD)
+    to_two = scale * math.log2(math.e)
+    nt = (((1,), (1,)), ((), ()))
+
+    def one_block(turn, carry):
+        page, at_block = lax.div(turn, blocks), lax.rem(turn, blocks)
+        block = lax.rem(y + 1 + at_block, blocks)
+        length = jnp.where(page == 0, lengths[0], lengths[1])
+
+        def key_part(i):
+            at = i * step
+            if at < lat:
+                return k_ref[page, pl.ds(at, step), :]
+            return kv_ref[pl.ds(pl.multiple_of(page * lat + at - lat, step), step), pl.ds(0, HD)]
+
+        def value_part(i):
+            at = i * step
+            if at < lat:
+                return v_ref[page, pl.ds(at, step), :]
+            return kv_ref[pl.ds(pl.multiple_of(page * lat + at - lat, step), step), pl.ds(HD, HD)]
+
+        @pl.when(at_block == 0)
+        def _():
+            for i in range(steps):
+                kt[:, pl.ds(i * step, step)] = key_part(i).T
+                vt[:, pl.ds(i * step, step)] = value_part(i).T
+            kacc[...] = jnp.zeros_like(kacc)
+            vacc[...] = jnp.zeros_like(vacc)
+
+        places = pl.ds(pl.multiple_of(block * bq, bq), bq)
+        q, g = q_ref[page, places, :], g_ref[page, places, :]
+        highest = jnp.full((1, bq), -jnp.inf, F32)
+        for i in range(steps):
+            scores = lax.dot_general(key_part(i), q, nt, preferred_element_type=F32)
+            if i * step >= lat:
+                at = i * step - lat + lax.broadcasted_iota(jnp.int32, (step, bq), 0)
+                scores = jnp.where(at < length, scores, -jnp.inf)
+            highest = jnp.maximum(highest, jnp.max(scores, axis=0, keepdims=True))
+            e_s[pl.ds(i * step, step), :] = scores
+        top = highest * to_two
+        weight = jnp.zeros((1, bq), F32)
+        weighted = jnp.zeros((1, bq), F32)
+        for i in range(steps):
+            raised = jnp.exp2(e_s[pl.ds(i * step, step), :] * to_two - top)
+            prob_grad = lax.dot_general(value_part(i), g, nt, preferred_element_type=F32)
+            weight = weight + jnp.sum(raised, axis=0, keepdims=True)
+            weighted = weighted + jnp.sum(raised * prob_grad, axis=0, keepdims=True)
+            e_s[pl.ds(i * step, step), :] = raised
+            d_s[pl.ds(i * step, step), :] = prob_grad
+        inverse = 1.0 / weight
+        centre = weighted * inverse
+        scaled = inverse * scale
+        att_t = jnp.zeros((HD, bq), F32)
+        qg_t = jnp.zeros((HD, bq), F32)
+        for i in range(steps):
+            at = pl.ds(i * step, step)
+            raised = e_s[at, :]
+            soft_low = (raised * inverse).astype(BF)
+            score_grad = (raised * scaled * (d_s[at, :] - centre)).astype(BF)
+            att_t = att_t + jnp.dot(vt[:, at], soft_low, preferred_element_type=F32)
+            qg_t = qg_t + jnp.dot(kt[:, at], score_grad, preferred_element_type=F32)
+            vacc[at, :] += jnp.dot(soft_low, g, preferred_element_type=F32)
+            kacc[at, :] += jnp.dot(score_grad, q, preferred_element_type=F32)
+        att[page, places, :] = att_t.T.astype(BF)
+        qg[page, places, :] = qg_t.T.astype(BF)
+        for z in range(ZN):
+            to = block * ZN + z
+
+            @pl.when(to != s)
+            def _():
+                out(0, page, to, s).start()
+                out(1, page, to, s).start()
+
+        @pl.when(at_block == blocks - 1)
+        def _():
+            kg[page] = kacc[pl.ds(0, lat), :].astype(BF)
+            vg[page] = vacc[pl.ds(0, lat), :].astype(BF)
+            columns = pl.ds(pl.multiple_of(page * lat, lat), lat)
+            pg_t[pl.ds(0, HD), columns] = kacc[pl.ds(lat, lat), :].T.astype(BF)
+            pg_t[pl.ds(HD, HD), columns] = vacc[pl.ds(lat, lat), :].T.astype(BF)
+
+            @pl.when(page < pages - 1)
+            def _():
+                send_key_grads(page)
+
+        return carry
+
+    def send_key_grads(page):
+        def one(k, carry):
+            to = lax.rem(s + k, n)
+            out(2, page, to, s).start()
+            out(3, page, to, s).start()
+            return carry
+
+        lax.fori_loop(1, n, one, 0)
+
+    lax.fori_loop(0, pages * blocks, one_block, 0)
 
     def mate(k):
         return high * group + lax.rem(j + k, group)
 
-    def piece(array, t):
-        return array.at[pl.ds(pl.multiple_of(t * chunk, chunk), chunk), :]
+    def summed(t):
+        columns = pl.ds(pl.multiple_of(t * chunk, chunk), chunk)
+        return jnp.dot(pg_t[...], rows[:, columns], preferred_element_type=F32)
 
     def scatter(k):
-        t = lax.rem(j + k, group)
         return push(
-            piece(partial, t), parts.at[group - k], rsend.at[k], rrecv.at[k], "lang", mate(k)
+            outbound.at[k], parts.at[group - k], rsend.at[k], rrecv.at[k], "lang", mate(k)
         )
 
-    def spread(k):
-        return push(done, piece(total, j), asend.at[k], arecv.at[k], "lang", mate(k))
-
-    for k in range(1, group):
+    def piece(t):
+        return total.at[pl.ds(pl.multiple_of(t * chunk, chunk), chunk), :]
+
+    def spread(k, t):
+        return push(done, piece(t), asend.at[k], arecv.at[k], "lang", mate(k))
+
+    fetch.wait()
+
+    def one_part(k, carry):
+        outbound[k] = summed(lax.rem(j + k, group)).astype(BF)
         scatter(k).start()
-    sbegin()
-    for copy in own:
-        copy.start()
-    keep = pltpu.make_async_copy(piece(partial, j), parts.at[0], own_sem.at[len(pieces)])
-    keep.start()
-    keep.wait()
+        return carry
+
+    lax.fori_loop(1, group, one_part, 0)
+    send_key_grads(pages - 1)
+    own = []
+    for i in range(4):
+        own.append(
+            pltpu.make_async_copy(
+                sources[i].at[:, pl.ds(pl.multiple_of(s * part, part), part), :],
+                landings[i].at[:, :, pl.ds(pl.multiple_of(s * HD, HD), HD)],
+                own_sem.at[i],
+            )
+        )
+        own[-1].start()
+    acc = summed(j)
     for k in range(1, group):
         scatter(k).wait()
-    acc = parts[0].astype(F32)
-    for k in range(1, group):
-        acc = acc + parts[k].astype(F32)
+        acc = acc + parts[group - k].astype(F32)
     mine[...] = acc.astype(BF)
-    other = lax.rem(l + group, 2 * group)
-    cross = push(mine, pair, psend.at[0], precv.at[0], "lang", other)
+    cross = push(
+        mine, pair, psend.at[0], precv.at[0], "lang", lax.rem(l + group, 2 * group)
+    )
     cross.start()
     cross.wait()
-    done[...] = (mine[...].astype(F32) + pair[...].astype(F32)).astype(BF)
+    done[...] = (mine[...].astype(F32) + pair[...].astype(F32)).T.astype(BF)
     for k in range(1, group):
-        spread(k).start()
-    last = pltpu.make_async_copy(done, piece(total, j), own_sem.at[len(pieces)])
+        spread(k, j).start()
+    last = pltpu.make_async_copy(done, piece(j), own_sem.at[4])
     last.start()
-    sfinish()
+
+    def ended(k, carry):
+        other = lax.rem(s + k, n)
+        for i in range(4):
+            for page in range(pages):
+                out(i, page, other, other).wait()
+        return carry
+
+    lax.fori_loop(1, n, ended, 0)
     for copy in own:
         copy.wait()
     last.wait()
     for k in range(1, group):
-        spread(k).wait_send()
-        t = lax.rem(j + group - k, group)
-        push(done, piece(total, t), asend.at[k], arecv.at[k], "lang", mate(k)).wait_recv()
-
-
-def attention_kernel(
-    lengths, q_ref, g_ref, kl_ref, vl_ref, kp_ref, vp_ref,
-    att_ref, qg_ref, kg_ref, vg_ref, pg_ref,
-    kt, vt, kacc, vacc, e_s, d_s,
-):
-    page, block = pl.program_id(0), pl.program_id(1)
-    length = lengths[page]
-    lat = kl_ref.shape[1]
-    keys_all = 2 * lat
-    step = 256
-    bq = q_ref.shape[1]
-    scale = 1.0 / math.sqrt(HD)
-    to_two = scale * math.log2(math.e)
-
-    def key_part(i):
-        at = i * step
-        return kl_ref[0, pl.ds(at, step), :] if at < lat else kp_ref[pl.ds(at - lat, step), :]
-
-    def value_part(i):
-        at = i * step
-        return vl_ref[0, pl.ds(at, step), :] if at < lat else vp_ref[pl.ds(at - lat, step), :]
-
-    steps = keys_all // step
-
-    @pl.when(block == 0)
-    def _():
-        for i in range(steps):
-            kt[:, pl.ds(i * step, step)] = key_part(i).T
-            vt[:, pl.ds(i * step, step)] = value_part(i).T
-        kacc[...] = jnp.zeros_like(kacc)
-        vacc[...] = jnp.zeros_like(vacc)
-
-    q, g = q_ref[0], g_ref[0]
-    nt = (((1,), (1,)), ((), ()))
-    highest = jnp.full((1, bq), -jnp.inf, F32)
-    for i in range(steps):
-        scores = lax.dot_general(key_part(i), q, nt, preferred_element_type=F32)
-        if i * step >= lat:
-            at = i * step - lat + lax.broadcasted_iota(jnp.int32, (step, bq), 0)
-            scores = jnp.where(at < length, scores, -jnp.inf)
-        highest = jnp.maximum(highest, jnp.max(scores, axis=0, keepdims=True))
-        e_s[pl.ds(i * step, step), :] = scores
-    top = highest * to_two
-    total = jnp.zeros((1, bq), F32)
-    weighted = jnp.zeros((1, bq), F32)
-    for i in range(steps):
-        raised = jnp.exp2(e_s[pl.ds(i * step, step), :] * to_two - top)
-        prob_grad = lax.dot_general(value_part(i), g, nt, preferred_element_type=F32)
-        total = total + jnp.sum(raised, axis=0, keepdims=True)
-        weighted = weighted + jnp.sum(raised * prob_grad, axis=0, keepdims=True)
-        e_s[pl.ds(i * step, step), :] = raised
-        d_s[pl.ds(i * step, step), :] = prob_grad
-    inverse = 1.0 / total
-    centre = weighted * inverse
-    scaled = inverse * scale
-    att_t = jnp.zeros((HD, bq), F32)
-    qg_t = jnp.zeros((HD, bq), F32)
-    for i in range(steps):
-        at = pl.ds(i * step, step)
-        raised = e_s[at, :]
-        soft_low = (raised * inverse).astype(BF)
-        score_grad = (raised * scaled * (d_s[at, :] - centre)).astype(BF)
-        att_t = att_t + jnp.dot(vt[:, at], soft_low, preferred_element_type=F32)
-        qg_t = qg_t + jnp.dot(kt[:, at], score_grad, preferred_element_type=F32)
-        vacc[at, :] += jnp.dot(soft_low, g, preferred_element_type=F32)
-        kacc[at, :] += jnp.dot(score_grad, q, preferred_element_type=F32)
-    att_ref[0] = att_t.T.astype(BF)
-    qg_ref[0] = qg_t.T.astype(BF)
-
-    @pl.when(block == pl.num_programs(1) - 1)
-    def _():
-        kg_ref[0] = kacc[pl.ds(0, lat), :].astype(BF)
-        vg_ref[0] = vacc[pl.ds(0, lat), :].astype(BF)
-        pg_ref[:, pl.ds(0, HD)] = kacc[pl.ds(lat, lat), :].astype(BF)
-        pg_ref[:, pl.ds(HD, HD)] = vacc[pl.ds(lat, lat), :].astype(BF)
-
-
-def attention(lengths, q, g, k, v, kv):
-    pages, lat, _ = q.shape
-    bq = 256
-    row = pl.BlockSpec((1, bq, HD), lambda p, b, _: (p, b, 0))
-    full = pl.BlockSpec((1, lat, HD), lambda p, b, _: (p, 0, 0))
-    key = pl.BlockSpec((lat, HD), lambda p, b, _: (p, 0))
-    value = pl.BlockSpec((lat, HD), lambda p, b, _: (p, 1))
-    both = pl.BlockSpec((lat, 2 * HD), lambda p, b, _: (p, 0))
-    shape = jax.ShapeDtypeStruct((pages, lat, HD), BF)
-    return pl.pallas_call(
-        attention_kernel,
-        grid_spec=pltpu.PrefetchScalarGridSpec(
-            num_scalar_prefetch=1,
-            grid=(pages, lat // bq),
-            in_specs=[row, row, full, full, key, value],
-            out_specs=[row, row, full, full, both],
-            scratch_shapes=[
-                pltpu.VMEM((HD, 2 * lat), BF),
-                pltpu.VMEM((HD, 2 * lat), BF),
-                pltpu.VMEM((2 * lat, HD), F32),
-                pltpu.VMEM((2 * lat, HD), F32),
-                pltpu.VMEM((2 * lat, bq), F32),
-                pltpu.VMEM((2 * lat, bq), F32),
-            ],
-        ),
-        out_shape=[shape] * 4 + [jax.ShapeDtypeStruct((pages * lat, 2 * HD), BF)],
-        compiler_params=pltpu.CompilerParams(vmem_limit_bytes=48 << 20),
-    )(lengths, q, g, k, v, kv, kv)
-
-
-def remote(body, number, out_shape, scratch, *operands, in_vmem=()):
+        spread(k, lax.rem(j + group - k, group)).wait()
+
+
+def remote(body, number, out_shape, scratch, *operands, in_vmem=(), in_smem=()):
     return pl.pallas_call(
         body,
         out_shape=out_shape,
         in_specs=[
-            pl.BlockSpec(memory_space=pltpu.VMEM) if i in in_vmem else ANY
+            pl.BlockSpec(memory_space=pltpu.SMEM)
+            if i in in_smem
+            else pl.BlockSpec(memory_space=pltpu.VMEM)
+            if i in in_vmem
+            else ANY
             for i in range(len(operands))
         ],
         out_specs=[ANY] * len(out_shape),
         scratch_shapes=scratch,
         compiler_params=pltpu.CompilerParams(
-            collective_id=number, has_side_effects=True, vmem_limit_bytes=32 << 20
+            collective_id=number, has_side_effects=True, vmem_limit_bytes=48 << 20
         ),
     )(*operands)
 
@@ -638,27 +660,37 @@
     kv = jnp.dot(
         group_rows, w_kv.reshape(model_width, 2 * HD), preferred_element_type=F32
     ).astype(BF)
-    att, qg, kg, vg, prompt_grad = attention(prompt_lengths, qh, gh, kh, vh, kv)
-    partial = lax.dot_general(
-        group_rows, prompt_grad, (((0,), (0,)), ((), ())), preferred_element_type=F32
-    ).astype(BF)
     half = lang_count // 2
     chunk = model_width // half
+    bq = lat // YN
     att_rows, latent, total = remote(
-        back_kernel,
+        attend_kernel,
         4,
         [
             sds(latent_q.shape, BF),
             sds((3,) + latent_q.shape, BF),
-            sds(partial.shape, BF),
+            sds((model_width, 2 * HD), BF),
         ],
         [
-            pltpu.VMEM((half, chunk, 2 * HD), BF),
+            pltpu.VMEM(group_rows.shape, BF),
+            pltpu.VMEM((pages, lat, HD), BF),
+            pltpu.VMEM((pages, lat, HD), BF),
+            pltpu.VMEM((pages, lat, HD), BF),
+            pltpu.VMEM((pages, lat, HD), BF),
+            pltpu.VMEM((2 * HD, pages * lat), BF),
+            pltpu.VMEM((HD, 2 * lat), BF),
+            pltpu.VMEM((HD, 2 * lat), BF),
+            pltpu.VMEM((2 * lat, HD), F32),
+            pltpu.VMEM((2 * lat, HD), F32),
+            pltpu.VMEM((2 * lat, bq), F32),
+            pltpu.VMEM((2 * lat, bq), F32),
+            pltpu.VMEM((half, 2 * HD, chunk), BF),
+            pltpu.VMEM((half, 2 * HD, chunk), BF),
+            pltpu.VMEM((2 * HD, chunk), BF),
+            pltpu.VMEM((2 * HD, chunk), BF),
             pltpu.VMEM((chunk, 2 * HD), BF),
-            pltpu.VMEM((chunk, 2 * HD), BF),
-            pltpu.VMEM((chunk, 2 * HD), BF),
-            DMA((4, seq_count)),
-            DMA((4, seq_count)),
+            DMA((4, pages, seq_count)),
+            DMA((4, pages, seq_count)),
             DMA((5,)),
             DMA((half,)),
             DMA((half,)),
@@ -667,11 +699,15 @@
             DMA((half,)),
             DMA((half,)),
         ],
-        att,
-        qg,
-        kg,
-        vg,
-        partial,
+        prompt_lengths,
+        qh,
+        gh,
+        kh,
+        vh,
+        kv,
+        group_rows,
+        in_vmem=(1, 2, 3, 4, 5),
+        in_smem=(0,),
     )
     grad_wkv = total.astype(F32).reshape(model_width, 2, HD)
     return (att_rows, latent, grad_wkv)

time: 343 us -> 330 us (0.962)
  Pallas kernels: 319 us -> 303 us
  matrix products: 10.7 us -> 14.9 us
    pallas_call x1 -> x0, Pallas kernels: 21.2 us -> none  [attention(): pl.pallas_call(attention_kernel, grid_spec=pltpu.PrefetchScalarGridSpec(n...]
    pallas_call x3, Pallas kernels: 298 us -> 303 us  [remote(): pl.pallas_call(body, out_shape=out_shape, in_specs=[pl.BlockSpec(memory_s...]
where the time goes in v3:
time: 330 us; the launch traced here: 329 us
  Pallas kernels  303 us (92%)
  matrix products  14.9 us (5%)
  local copies, waits for them, and re-layouts  7.88 us (2%)
    pallas_call x3, Pallas kernels, remote(): pl.pallas_call(body, out_shape=out_shape, in_specs=[pl.BlockSpec(memory_s...  303 us

profile of v3, /device:TPU:1, one launch (start us, length us, event | category | flops | bytes accessed | tf_op | source)
XLA Modules:
  0.0 329.0 jit_solution(15638526215569821566)
XLA Ops:
  0.6 0.0 copy-start
  0.6 0.8 copy.32
  1.5 0.1 eq.56
  1.6 0.1 eq.52
  1.8 0.6 reduce-window.6
  2.4 0.2 slice_reduce_fusion
  2.6 0.1 fusion.16
  2.7 0.1 reduce_sum.12
  2.8 0.1 copy.35
  2.9 0.7 multiply_add_fusion
  3.7 0.8 copy.36.gates
  4.4 0.1 fusion.13.pick
  4.6 0.0 copy-start.1
  4.6 1.2 pad_maximum_fusion.pack
  5.8 0.6 convolution_convert_fusion
  6.4 116.7 %shard_map.139 = (bf16[2112,2048]{1,0:T(8,128)(2,1)}, bf16[16,24,2048]{2,1,0:T(8,128)(2,1)S(1)}, bf16[2,1024,128]{2,1,0:T(8,128)(2,1)S(1)}, bf16[2,1024,128]{2,1,0:T(8,128)(2,1)S(1)}) custom-call(bf16[2112,128]{1,0:T(8,128)(2,1)S(1)} %pad_maximum_fusion.pack, bf16[16,24,2048]{2,1,0:T(8,128)(2,1)S(1)} %bitcast.38, bf16[2,64,2048]{2,1,0:T(8,128)(2,1)S(1)} %copy-done.1, ...), custom_call_target="tpu_custom_call" | custom-call | tf_op jit(solution)/shard_map/pallas_call | solution.py:567
  123.1 5.3 %fusion = f32[384,1408]{1,0:T(8,128)S(1)} fusion(bf16[384,2048]{1,0:T(8,128)(2,1)S(1)} %bitcast.40, bf16[2112,2048]{1,0:T(8,128)(2,1)} %get-tuple-element.16), kind=kOutput, calls=%fused_computation | convolution fusion | flops 2214592512 | bytes 9502720 | tf_op jit(solution)/shard_map/dot_general | solution.py:635
  128.4 3.3 %fusion.4 = bf16[384,2048]{1,0:T(8,128)(2,1)S(1)} fusion(bf16[2112,2048]{1,0:T(8,128)(2,1)} %get-tuple-element.16, f32[384,1408]{1,0:T(8,128)S(1)} %fusion), kind=kOutput, calls=%fused_computation.4 | convolution fusion | flops 1109704704 | bytes 6815744 | tf_op jit(solution)/shard_map/dot_general | solution.py:637
  131.8 117.3 %shard_map.140 = (bf16[2048,2048]{1,0:T(8,128)(2,1)}, bf16[2,1024,128]{2,1,0:T(8,128)(2,1)S(1)}, bf16[2,1024,128]{2,1,0:T(8,128)(2,1)S(1)}) custom-call(bf16[16,24,2048]{2,1,0:T(8,128)(2,1)S(1)} %bitcast.39, bf16[2,128,384]{2,1,0:T(8,128)(2,1)S(1)} %fusion.13.pick, f32[128,2]{1,0:T(8,128)S(1)} %copy.36.gates, bf16[2,64,2048]{2,1,0:T(8,128)(2,1)S(1)} %copy-done.3, ...), custom_call_target="tpu_custom_call" | custom-call | tf_op jit(solution)/shard_map/pallas_call | solution.py:567
  249.1 5.7 %convolution_convert_fusion.1.kv_ref = bf16[2048,256]{1,0:T(8,128)(2,1)S(1)} fusion(bf16[2048,2048]{1,0:T(8,128)(2,1)} %get-tuple-element.19.rows_hbm, bf16[256,8,2,128]{3,2,1,0:T(2,128)(2,1)S(1)} %bitcast.45), kind=kOutput, calls=%fused_computation.6 | convolution fusion | flops 2148007936 | bytes 10485760 | tf_op jit(solution)/shard_map/dot_general | solution.py:660
  254.9 68.6 %shard_map.141 = (bf16[2,64,2048]{2,1,0:T(8,128)(2,1)S(1)}, bf16[3,2,64,2048]{3,2,1,0:T(8,128)(2,1)}, bf16[2048,256]{1,0:T(8,128)(2,1)S(1)}) custom-call(s32[2]{0:T(128)S(1)} %copy-done.5, bf16[2,1024,128]{2,1,0:T(8,128)(2,1)S(1)} %get-tuple-element.13.q_ref, bf16[2,1024,128]{2,1,0:T(8,128)(2,1)S(1)} %get-tuple-element.14.g_ref, ...), custom_call_target="tpu_custom_call" | custom-call | tf_op jit(solution)/shard_map/pallas_call | solution.py:567
  323.5 2.0 reshape.59
  325.5 0.8 copy.46
  326.3 2.7 copy.47
  (16 shorter events, 0.1 us)
Async XLA Ops:
  0.6 5.2 %copy-start = (bf16[128,2048]{1,0:T(8,128)(2,1)S(1)}, bf16[128,2048]{1,0:T(8,128)(2,1)}, u32[]{:S(2)}) copy-start(bf16[128,2048]{1,0:T(8,128)(2,1)} %param.12) | copy-start | bytes 1572868
  4.6 1.8 copy-start.1
  4.6 1.8 copy-start.2
  128.4 3.4 %copy-start.3 = (bf16[2,64,2048]{2,1,0:T(8,128)(2,1)S(1)}, bf16[2,64,2048]{2,1,0:T(8,128)(2,1)}, u32[]{:S(2)}) copy-start(bf16[2,64,2048]{2,1,0:T(8,128)(2,1)} %k.1) | copy-start | bytes 1572868
  128.4 3.4 %copy-start.4 = (bf16[2,64,2048]{2,1,0:T(8,128)(2,1)S(1)}, bf16[2,64,2048]{2,1,0:T(8,128)(2,1)}, u32[]{:S(2)}) copy-start(bf16[2,64,2048]{2,1,0:T(8,128)(2,1)} %v.1) | copy-start | bytes 1572868
  131.7 117.4 %copy-start.6 = (bf16[2048,2,128]{2,1,0:T(2,128)(2,1)S(1)}, bf16[2048,2,128]{2,1,0:T(2,128)(2,1)}, u32[]{:S(2)}) copy-start(bf16[2048,2,128]{2,1,0:T(2,128)(2,1)} %param.18) | copy-start | bytes 3145732
  249.1 5.8 %copy-start.5 = (s32[2]{0:T(128)S(1)}, s32[2]{0:T(128)}, u32[]{:S(2)}) copy-start(s32[2]{0:T(128)} %lengths.1) | copy-start | bytes 28

commit v4 on v3

--- a/solution.py
+++ b/solution.py
@@ -156,25 +156,26 @@
         else:
             each_side(t, lambda col, to_right: pass_on(c, col))
 
+    def landed(c):
+        for col in range(ZN):
+            for copy in forwards(c, col):
+                copy.wait_recv()
+
     def finish(c):
+        for col in range(ZN):
+            for copy in across(c, col, False) + forwards(c, col):
+                copy.wait_send()
         for to_right in (True, False):
             on_way(to_right, lambda: along(c, z, to_right, True).wait_send())
-        for copy in across(c, z, True):
-            copy.wait_send()
-        for copy in forwards(c, z):
-            copy.wait()
         for t in range(1, ZN):
-
-            def ended(col, to_right):
-                on_way(to_right, lambda: along(c, col, to_right, False).wait_send())
-                for copy in across(c, col, False):
-                    copy.wait_send()
-                for copy in forwards(c, col):
-                    copy.wait()
-
-            each_side(t, ended)
-
-    return begin, step, relay, finish
+            each_side(
+                t,
+                lambda col, to_right: on_way(
+                    to_right, lambda: along(c, col, to_right, False).wait_send()
+                ),
+            )
+
+    return begin, step, relay, landed, finish
 
 
 def swap_steps(axis, pieces, send, recv):
@@ -217,84 +218,44 @@
     return [(source(a), landing(b)) for a, b in pairs]
 
 
-def dispatch_kernel(
-    pack, outgoing, q, g, whole, arrived, qh, gh, send, recv, lsend, lrecv, own_sem, *gsems
-):
-    s = lax.axis_index("seq")
-    pieces = latent_pieces([(q, qh), (g, gh)])
-    lbegin, lfinish = swap_steps("seq", pieces, lsend, lrecv)
-    me = lax.axis_index("lang")
-    chunks = 3
-    size = pack.shape[0] // chunks
-
-    def view(c, shard, half):
-        columns = pl.ds(pl.multiple_of(shard * HD, HD), HD)
-        if half is None:
-            return whole.at[pl.ds(c * size, size), columns]
-        rows = size // 2
-        return whole.at[pl.ds(c * size + half * rows, rows), columns]
-
-    begin, step, relay, finish = gather_steps(
-        lambda c: pack.at[pl.ds(c * size, size), :], view, gsems
-    )
-    sbegin, sfinish = swap_steps(
-        "lang", [(lambda t: outgoing.at[t], lambda m: arrived.at[m])], send, recv
-    )
-    own = [
-        pltpu.make_async_copy(
-            pack, whole.at[:, pl.ds(pl.multiple_of(s * HD, HD), HD)], own_sem.at[0]
-        ),
-        pltpu.make_async_copy(outgoing.at[me], arrived.at[me], own_sem.at[1]),
-    ]
-    for i, (a, b) in enumerate(pieces):
-        own.append(pltpu.make_async_copy(a(s), b(s), own_sem.at[i + 2]))
-    greet(["lang", "seq"])
-    for c in range(chunks):
-        begin(c)
-    sbegin()
-    for copy in own:
-        copy.start()
-    for t in range(1, ZN):
-        for c in range(chunks):
-            step(c, t)
-            relay(c, t - 1)
-        if t == 1:
-            lbegin()
-    for c in range(chunks):
-        relay(c, ZN - 1)
-    sfinish()
-    lfinish()
-    for c in range(chunks):
-        finish(c)
-    for copy in own:
-        copy.wait()
-
-
-def prompt_kernel(
-    results, pick, gates, k, v, rows, kh, vh,
-    returned, mixed, rsend, rrecv, send, recv, own_sem, *gsems,
+def encode(
+    w_parts, outgoing, pick, gates, w_kv, latents, heads, kv, rows,
+    whole, arrived, tokens, gate_up, hidden, results, returned, mixed,
+    dsend, drecv, rsend, rrecv, lsend, lrecv, own_sem, wsems, msems,
 ):
     s = lax.axis_index("seq")
     me = lax.axis_index("lang")
     count, width = mixed.shape
-    chunks = rsend.shape[0]
-    wide = width // chunks
-
-    def view(c, shard, half):
+    size = w_parts[0].shape[0]
+    wide = width // CHUNKS
+    experts, capacity, _ = arrived.shape
+
+    def wview(c, shard, half):
+        columns = pl.ds(pl.multiple_of(shard * HD, HD), HD)
+        if half is None:
+            return whole.at[pl.ds(c * size, size), columns]
+        part = size // 2
+        return whole.at[pl.ds(c * size + half * part, part), columns]
+
+    def mview(c, shard, half):
         columns = pl.ds(c * wide, wide)
         if half is None:
             return rows.at[pl.ds(pl.multiple_of(shard * count, count), count), columns]
-        size = count // 2
-        at = pl.multiple_of(shard * count + half * size, size)
-        return rows.at[pl.ds(at, size), columns]
-
-    pieces = latent_pieces([(k, kh), (v, vh)])
-    begin, step, relay, finish = gather_steps(
-        lambda c: mixed.at[:, pl.ds(c * wide, wide)], view, gsems
+        part = count // 2
+        at = pl.multiple_of(shard * count + half * part, part)
+        return rows.at[pl.ds(at, part), columns]
+
+    wbegin, wstep, wrelay, wlanded, wfinish = gather_steps(lambda c: w_parts[c], wview, wsems)
+    begin, step, relay, landed, finish = gather_steps(
+        lambda c: mixed.at[:, pl.ds(c * wide, wide)], mview, msems
     )
+    dbegin, dfinish = swap_steps(
+        "lang", [(lambda t: outgoing.at[t], lambda m: arrived.at[m])], dsend, drecv
+    )
+    pieces = latent_pieces(list(zip(latents, heads)))
     swaps = [
-        swap_steps("seq", [pieces[i]], send.at[pl.ds(i, 1)], recv.at[pl.ds(i, 1)])
-        for i in range(2)
+        swap_steps("seq", [pieces[i]], lsend.at[pl.ds(i, 1)], lrecv.at[pl.ds(i, 1)])
+        for i in range(4)
     ]
 
     def back(c):
@@ -306,43 +267,101 @@
             rrecv.at[pl.ds(c, 1)],
         )
 
-    backs = [back(c) for c in range(chunks)]
-    own = [pltpu.make_async_copy(results.at[me], returned.at[me], own_sem.at[0])]
+    backs = [back(c) for c in range(CHUNKS)]
+    own = [pltpu.make_async_copy(outgoing.at[me], arrived.at[me], own_sem.at[0])]
+    for c in range(3):
+        own.append(pltpu.make_async_copy(w_parts[c], wview(c, s, None), own_sem.at[1 + c]))
     for i, (a, b) in enumerate(pieces):
-        own.append(pltpu.make_async_copy(a(s), b(s), own_sem.at[i + 1]))
-    greet(["seq", "lang"])
+        own.append(pltpu.make_async_copy(a(s), b(s), own_sem.at[4 + i]))
+    for c in range(3):
+        wbegin(c)
+    dbegin()
     for copy in own:
         copy.start()
-    for c in range(chunks):
+    for t in range(1, ZN):
+        for c in range(3):
+            wstep(c, t)
+            wrelay(c, t - 1)
+        if t == 1:
+            swaps[0][0]()
+            swaps[1][0]()
+        if t == ZN - 1:
+            swaps[2][0]()
+            swaps[3][0]()
+    for c in range(3):
+        wrelay(c, ZN - 1)
+    dfinish()
+    for copy in own:
+        copy.wait()
+    for at in range(CHUNKS):
+        columns = pl.ds(at * wide, wide)
+        slots = arrived[:, :, columns].astype(F32)
+        tokens[:, columns] = slots.reshape(experts * capacity, wide).astype(BF)
+    wlanded(0)
+    wlanded(1)
+    gate_up[...] = jnp.zeros_like(gate_up)
+    tile = 512
+
+    def one_depth(i, carry):
+        columns = pl.ds(pl.multiple_of(i * tile, tile), tile)
+        gate_up[...] += lax.dot_general(
+            tokens[:, columns],
+            whole[pl.ds(0, 2 * size), columns],
+            (((1,), (1,)), ((), ())),
+            preferred_element_type=F32,
+        )
+        return carry
+
+    lax.fori_loop(0, width // tile, one_depth, 0)
+    gate = gate_up[:, :size]
+    hidden[...] = (gate / (1.0 + jnp.exp(-gate)) * gate_up[:, size:]).astype(BF)
+    wlanded(2)
+    mates = []
+    for c in range(CHUNKS):
+
+        def one_tile(i, carry):
+            columns = pl.ds(pl.multiple_of(c * wide + i * tile, tile), tile)
+            result = jnp.dot(
+                hidden[...], whole[pl.ds(2 * size, size), columns], preferred_element_type=F32
+            )
+            results[:, :, columns] = result.reshape(experts, capacity, tile).astype(BF)
+            return carry
+
+        lax.fori_loop(0, wide // tile, one_tile, 0)
         backs[c][0]()
-    own[0].wait()
+        columns = pl.ds(c * wide, wide)
+        mates.append(
+            pltpu.make_async_copy(
+                results.at[me, :, columns], returned.at[me, :, columns], own_sem.at[c]
+            )
+        )
+        mates[-1].start()
     places = []
 
     def mix(c):
         backs[c][1]()
+        mates[c].wait()
         columns = pl.ds(c * wide, wide)
         slots = returned[:, :, columns].astype(F32)
-        slots = slots.reshape(slots.shape[0] * slots.shape[1], wide).astype(BF)
+        slots = slots.reshape(experts * capacity, wide).astype(BF)
         total = jnp.zeros((count, wide), F32)
         for which in range(pick.shape[0]):
             picked = jnp.dot(pick[which], slots, preferred_element_type=F32)
             total = total + gates[:, which : which + 1] * picked
         mixed[:, columns] = total.astype(BF)
         place = pltpu.make_async_copy(
-            mixed.at[:, columns], view(c, s, None), own_sem.at[3 + c]
+            mixed.at[:, columns], mview(c, s, None), own_sem.at[CHUNKS + c]
         )
         place.start()
         places.append(place)
         begin(c)
 
     mix(0)
-    swaps[0][0]()
     step(0, 1)
     mix(1)
     relay(0, 0)
     step(0, 2)
     step(1, 1)
-    swaps[1][0]()
     relay(0, 1)
     relay(1, 0)
     step(0, 3)
@@ -353,17 +372,56 @@
     relay(0, 3)
     relay(1, 2)
     relay(1, 3)
+    for copy in places:
+        copy.wait()
+    for c in range(CHUNKS):
+        landed(c)
+
+    def one_part(i, carry):
+        at = pl.ds(pl.multiple_of(i * 256, 256), 256)
+        kv[at, :] = jnp.dot(rows[at, :], w_kv[...], preferred_element_type=F32).astype(BF)
+        return carry
+
+    lax.fori_loop(0, rows.shape[0] // 256, one_part, 0)
     for swap in swaps:
         swap[1]()
-    for c in range(chunks):
+    for c in range(3):
+        wfinish(c)
+    for c in range(CHUNKS):
         finish(c)
-    for copy in own[1:] + places:
-        copy.wait()
-
-
-def attend_kernel(
-    lengths, q_ref, g_ref, k_ref, v_ref, kv_ref, rows_hbm, att_rows, latent, total,
-    rows, att, qg, kg, vg, pg_t, kt, vt, kacc, vacc, e_s, d_s,
+
+
+def whole_kernel(*refs):
+    refs = list(refs)
+
+    def take(n):
+        got = refs[:n]
+        del refs[:n]
+        return got
+
+    (lengths, pick, gates, w_kv) = take(4)
+    w_parts = take(3)
+    (outgoing,) = take(1)
+    latents = take(4)
+    outs = take(3)
+    heads = take(4)
+    kv, rows = take(2)
+    encode_scratch = take(8)
+    encode_sems = take(7)
+    wsems = take(11)
+    msems = take(11)
+    greet(["seq", "lang"])
+    encode(
+        w_parts, outgoing, pick, gates, w_kv, latents, heads, kv, rows,
+        *encode_scratch, *encode_sems, wsems, msems,
+    )
+    q, k, v, g = heads
+    attend(lengths, q, g, k, v, kv, rows, *outs, *refs)
+
+
+def attend(
+    lengths, q_ref, g_ref, k_ref, v_ref, kv_ref, rows, att_rows, latent, total,
+    att, qg, kg, vg, pg_t, kt, vt, kacc, vacc, e_s, d_s,
     outbound, parts, mine, pair, done,
     send, recv, own_sem, rsend, rrecv, psend, precv, asend, arecv,
 ):
@@ -378,9 +436,6 @@
     chunk = rows.shape[1] // group
     sources = [att, qg, kg, vg]
     landings = [att_rows, latent.at[0], latent.at[1], latent.at[2]]
-    fetch = pltpu.make_async_copy(rows_hbm, rows, own_sem.at[0])
-    fetch.start()
-    greet(["seq", "lang"])
 
     def out(i, page, to, frm):
         return push(
@@ -513,8 +568,6 @@
     def spread(k, t):
         return push(done, piece(t), asend.at[k], arecv.at[k], "lang", mate(k))
 
-    fetch.wait()
-
     def one_part(k, carry):
         outbound[k] = summed(lax.rem(j + k, group)).astype(BF)
         scatter(k).start()
@@ -578,7 +631,7 @@
         out_specs=[ANY] * len(out_shape),
         scratch_shapes=scratch,
         compiler_params=pltpu.CompilerParams(
-            collective_id=number, has_side_effects=True, vmem_limit_bytes=48 << 20
+            collective_id=number, has_side_effects=True, vmem_limit_bytes=60 << 20
         ),
     )(*operands)
 
@@ -609,74 +662,45 @@
     dispatch_mask = jnp.any(slot_ids[:, None, None] == targets[None, :, :], axis=2).astype(BF)
     outgoing = jnp.dot(dispatch_mask, prompt_rows, preferred_element_type=F32).astype(BF)
     outgoing = outgoing.reshape(experts_all, capacity, model_width)
-    pack = jnp.concatenate([w_gate[0].T, w_up[0].T, w_down[0]], axis=0)
+    pick = (targets.T[:, :, None] == slot_ids[None, None, :]).astype(BF)
     pages, part, _ = latent_q.shape
     lat = part * seq_count
-    heads = sds((pages, lat, HD), BF)
-    whole, arrived, qh, gh = remote(
-        dispatch_kernel,
-        1,
-        [sds((3 * ff, model_width), BF), sds(outgoing.shape, BF), heads, heads],
-        [
-            DMA((1, lang_count)),
-            DMA((1, lang_count)),
-            DMA((2, seq_count)),
-            DMA((2, seq_count)),
-            DMA((4,)),
-        ]
-        + gather_sems(3),
-        pack,
-        outgoing,
-        latent_q,
-        grad_out,
-    )
-    tokens = arrived.reshape(experts_all * capacity, model_width)
-    nt = (((1,), (1,)), ((), ()))
-    gate_up = lax.dot_general(tokens, whole[: 2 * ff], nt, preferred_element_type=F32)
-    hidden = (jax.nn.silu(gate_up[:, :ff]) * gate_up[:, ff:]).astype(BF)
-    results = jnp.dot(hidden, whole[2 * ff :], preferred_element_type=F32).astype(BF)
-    pick = (targets.T[:, :, None] == slot_ids[None, None, :]).astype(BF)
-    group_rows, kh, vh = remote(
-        prompt_kernel,
-        3,
-        [sds((rows_local * seq_count, model_width), BF)] + [heads] * 2,
-        [
-            pltpu.VMEM(outgoing.shape, BF),
-            pltpu.VMEM((rows_local, model_width), BF),
-            DMA((CHUNKS, lang_count)),
-            DMA((CHUNKS, lang_count)),
-            DMA((2, seq_count)),
-            DMA((2, seq_count)),
-            DMA((3 + CHUNKS,)),
-        ]
-        + gather_sems(CHUNKS),
-        results.reshape(outgoing.shape),
-        pick,
-        expert_gates,
-        latent_k,
-        latent_v,
-        in_vmem=(1, 2),
-    )
-    kv = jnp.dot(
-        group_rows, w_kv.reshape(model_width, 2 * HD), preferred_element_type=F32
-    ).astype(BF)
     half = lang_count // 2
     chunk = model_width // half
     bq = lat // YN
+    slots = experts_all * capacity
     att_rows, latent, total = remote(
-        attend_kernel,
-        4,
+        whole_kernel,
+        1,
         [
             sds(latent_q.shape, BF),
             sds((3,) + latent_q.shape, BF),
             sds((model_width, 2 * HD), BF),
         ],
-        [
-            pltpu.VMEM(group_rows.shape, BF),
-            pltpu.VMEM((pages, lat, HD), BF),
-            pltpu.VMEM((pages, lat, HD), BF),
-            pltpu.VMEM((pages, lat, HD), BF),
-            pltpu.VMEM((pages, lat, HD), BF),
+        [pltpu.VMEM((pages, lat, HD), BF)] * 4
+        + [
+            pltpu.VMEM((pages * lat, 2 * HD), BF),
+            pltpu.VMEM((rows_local * seq_count, model_width), BF),
+            pltpu.VMEM((3 * ff, model_width), BF),
+            pltpu.VMEM(outgoing.shape, BF),
+            pltpu.VMEM((slots, model_width), BF),
+            pltpu.VMEM((slots, 2 * ff), F32),
+            pltpu.VMEM((slots, ff), BF),
+            pltpu.VMEM(outgoing.shape, BF),
+            pltpu.VMEM(outgoing.shape, BF),
+            pltpu.VMEM((rows_local, model_width), BF),
+            DMA((1, lang_count)),
+            DMA((1, lang_count)),
+            DMA((CHUNKS, lang_count)),
+            DMA((CHUNKS, lang_count)),
+            DMA((4, seq_count)),
+            DMA((4, seq_count)),
+            DMA((8,)),
+        ]
+        + gather_sems(3)
+        + gather_sems(CHUNKS)
+        + [pltpu.VMEM((pages, lat, HD), BF)] * 4
+        + [
             pltpu.VMEM((2 * HD, pages * lat), BF),
             pltpu.VMEM((HD, 2 * lat), BF),
             pltpu.VMEM((HD, 2 * lat), BF),
@@ -700,13 +724,18 @@
             DMA((half,)),
         ],
         prompt_lengths,
-        qh,
-        gh,
-        kh,
-        vh,
-        kv,
-        group_rows,
-        in_vmem=(1, 2, 3, 4, 5),
+        pick,
+        expert_gates,
+        w_kv.reshape(model_width, 2 * HD),
+        w_gate[0].T,
+        w_up[0].T,
+        w_down[0],
+        outgoing,
+        latent_q,
+        latent_k,
+        latent_v,
+        grad_out,
+        in_vmem=(1, 2, 3),
         in_smem=(0,),
     )
     grad_wkv = total.astype(F32).reshape(model_width, 2, HD)

time: 330 us -> 312 us (0.945)
  matrix products: 14.9 us -> 1.7 us
  Pallas kernels: 303 us -> 297 us
    dot_general x3 -> x0, matrix products: 14.3 us -> none  [the longest x1 5.74 us: local(): jnp.dot(group_rows, w_kv.reshape(model_width, 2 * HD), preferred_element_...]
    pallas_call x3 -> x1, Pallas kernels: 303 us -> 297 us  [remote(): pl.pallas_call(body, out_shape=out_shape, in_specs=[pl.BlockSpec(memory_s...]
where the time goes in v4:
time: 312 us
  Pallas kernels  297 us (95%)
  local copies, waits for them, and re-layouts  10.4 us (3%)
    pallas_call x1, Pallas kernels, remote(): pl.pallas_call(body, out_shape=out_shape, in_specs=[pl.BlockSpec(memory_s...  297 us
    unnamed x11, local copies, waits for them, and re-layouts  6.53 us

profile of v4, /device:TPU:1, one launch (start us, length us, event | category | flops | bytes accessed | tf_op | source)
XLA Modules:
  0.0 312.2 jit_solution(10389332059715192462)
XLA Ops:
  0.6 0.0 copy-start
  0.6 0.8 copy.32
  1.5 0.1 eq.55
  1.6 0.1 eq.51
  1.8 0.6 reduce-window.6
  2.4 0.2 slice_reduce_fusion
  2.6 0.1 fusion.4
  2.7 0.1 reduce_sum.12
  2.8 0.1 copy.35
  2.9 0.7 multiply_add_fusion
  3.7 1.4 copy.36.refs_2_
  5.1 0.8 fusion.refs_1_
  5.8 2.3 copy.41
  8.2 0.0 copy-done
  8.2 1.7 convolution_convert_fusion
  9.9 297.2 %shard_map.139 = (bf16[2,64,2048]{2,1,0:T(8,128)(2,1)}, bf16[3,2,64,2048]{3,2,1,0:T(8,128)(2,1)}, bf16[2048,256]{1,0:T(8,128)(2,1)}) custom-call(s32[2]{0:T(128)} %refs_0_.1, bf16[2,128,384]{2,1,0:T(8,128)(2,1)} %fusion.refs_1_, f32[128,2]{1,0:T(8,128)} %copy.36.refs_2_, bf16[2048,256]{1,0:T(8,128)(2,1)} %bitcast.35, bf16[704,128]{1,0:T(8,128)(2,1)} %bitcast.37, ...), custom_call_target="tpu_custom_call" | custom-call | tf_op jit(solution)/shard_map/pallas_call | solution.py:620
  307.1 0.0 copy-start.2
  307.1 0.0 copy-start.1
  307.1 3.2 %reshape.51 = f32[2048,2,128]{2,1,0:T(2,128)} reshape(bf16[2048,256]{1,0:T(8,128)(2,1)} %get-tuple-element.8) | data formatting | bytes 3145728 | tf_op jit(solution)/shard_map/reshape | solution.py:741
  310.3 0.0 copy-done.2
  310.3 0.8 copy.44
  311.1 0.0 copy-done.1
  311.1 1.1 copy.45
  (4 shorter events, 0.1 us)
Async XLA Ops:
  0.6 7.6 %copy-start = (bf16[128,2048]{1,0:T(8,128)(2,1)S(1)}, bf16[128,2048]{1,0:T(8,128)(2,1)}, u32[]{:S(2)}) copy-start(bf16[128,2048]{1,0:T(8,128)(2,1)} %param.12) | copy-start | bytes 1572868
  307.1 3.2 %copy-start.2 = (bf16[2,64,2048]{2,1,0:T(8,128)(2,1)S(1)}, bf16[2,64,2048]{2,1,0:T(8,128)(2,1)}, u32[]{:S(2)}) copy-start(bf16[2,64,2048]{2,1,0:T(8,128)(2,1)} %get-tuple-element.12) | copy-start | bytes 1572868
  307.1 4.0 %copy-start.1 = (bf16[3,2,64,2048]{3,2,1,0:T(8,128)(2,1)S(1)}, bf16[3,2,64,2048]{3,2,1,0:T(8,128)(2,1)}, u32[]{:S(2)}) copy-start(bf16[3,2,64,2048]{3,2,1,0:T(8,128)(2,1)} %get-tuple-element.13) | copy-start | bytes 4718596

commit v5 on v4

--- a/solution.py
+++ b/solution.py
@@ -16,16 +16,6 @@
 ZN = 4
 CHUNKS = 2
 YN = 4
-
-
-def slot_targets(expert_ids, experts_all, capacity):
-    rows_local, picks = expert_ids.shape
-    flat_ids = expert_ids.reshape(rows_local * picks)
-    expert_range = jnp.arange(experts_all, dtype=jnp.int32)
-    onehot = (flat_ids[:, None] == expert_range[None, :]).astype(jnp.int32)
-    earlier = jnp.cumsum(onehot, axis=0) - onehot
-    slot_index = jnp.sum(earlier * onehot, axis=1)
-    return (flat_ids * capacity + slot_index).reshape(rows_local, picks)
 
 
 def push(src, dst, ssem, rsem, axis, target):
@@ -218,9 +208,36 @@
     return [(source(a), landing(b)) for a, b in pairs]
 
 
+def route(ids, gates, prompt_rows, masks, gate_columns, outgoing):
+    experts, capacity, width = outgoing.shape
+    count = prompt_rows.shape[0]
+    expert = lax.broadcasted_iota(jnp.int32, (experts, count), 0)
+    chosen = [expert == ids[k : k + 1, :] for k in range(2)]
+    named = jnp.where(jnp.logical_or(chosen[0], chosen[1]), 1.0, 0.0).astype(BF)
+    ahead = lax.broadcasted_iota(jnp.int32, (count, count), 0)
+    ahead = ahead < lax.broadcasted_iota(jnp.int32, (count, count), 1)
+    ahead = jnp.where(ahead, 1.0, 0.0).astype(BF)
+    earlier = jnp.dot(named, ahead, preferred_element_type=F32)
+    slot = lax.broadcasted_iota(jnp.int32, (experts * capacity, count), 0)
+    both = jnp.zeros((experts * capacity, count), F32)
+    for k in range(2):
+        order = jnp.sum(jnp.where(chosen[k], earlier, 0.0), axis=0, keepdims=True)
+        target = ids[k : k + 1, :] * capacity + order.astype(jnp.int32)
+        mask = jnp.where(slot == target, 1.0, 0.0)
+        masks[k] = mask.astype(BF)
+        both = both + mask
+        gate_columns[k] = jnp.broadcast_to(gates[k : k + 1, :], (count, count)).T
+    both = both.astype(BF)
+    tile = 512
+    for i in range(width // tile):
+        columns = pl.ds(i * tile, tile)
+        sent = jnp.dot(both, prompt_rows[:, columns], preferred_element_type=F32)
+        outgoing[:, :, columns] = sent.reshape(experts, capacity, tile).astype(BF)
+
+
 def encode(
-    w_parts, outgoing, pick, gates, w_kv, latents, heads, kv, rows,
-    whole, arrived, tokens, gate_up, hidden, results, returned, mixed,
+    w_parts, prompt_rows, ids, gates, w_kv, latents, heads, kv, rows,
+    masks, gate_columns, outgoing, whole, arrived, tokens, gate_up, hidden, results, returned, mixed,
     dsend, drecv, rsend, rrecv, lsend, lrecv, own_sem, wsems, msems,
 ):
     s = lax.axis_index("seq")
@@ -275,19 +292,21 @@
         own.append(pltpu.make_async_copy(a(s), b(s), own_sem.at[4 + i]))
     for c in range(3):
         wbegin(c)
-    dbegin()
-    for copy in own:
+    for copy in own[1:]:
         copy.start()
+    route(ids, gates, prompt_rows, masks, gate_columns, outgoing)
+    own[0].start()
     for t in range(1, ZN):
         for c in range(3):
             wstep(c, t)
             wrelay(c, t - 1)
         if t == 1:
+            dbegin()
+        if t == 2:
             swaps[0][0]()
+        if t == ZN - 1:
             swaps[1][0]()
-        if t == ZN - 1:
             swaps[2][0]()
-            swaps[3][0]()
     for c in range(3):
         wrelay(c, ZN - 1)
     dfinish()
@@ -345,9 +364,11 @@
         slots = returned[:, :, columns].astype(F32)
         slots = slots.reshape(experts * capacity, wide).astype(BF)
         total = jnp.zeros((count, wide), F32)
-        for which in range(pick.shape[0]):
-            picked = jnp.dot(pick[which], slots, preferred_element_type=F32)
-            total = total + gates[:, which : which + 1] * picked
+        for which in range(masks.shape[0]):
+            picked = lax.dot_general(
+                masks[which], slots, (((0,), (0,)), ((), ())), preferred_element_type=F32
+            )
+            total = total + gate_columns[which][:, 0:1] * picked
         mixed[:, columns] = total.astype(BF)
         place = pltpu.make_async_copy(
             mixed.at[:, columns], mview(c, s, None), own_sem.at[CHUNKS + c]
@@ -356,22 +377,17 @@
         places.append(place)
         begin(c)
 
-    mix(0)
-    step(0, 1)
-    mix(1)
-    relay(0, 0)
-    step(0, 2)
-    step(1, 1)
-    relay(0, 1)
-    relay(1, 0)
-    step(0, 3)
-    step(1, 2)
-    relay(0, 2)
-    relay(1, 1)
-    step(1, 3)
-    relay(0, 3)
-    relay(1, 2)
-    relay(1, 3)
+    for tick in range(CHUNKS + ZN):
+        if tick < CHUNKS:
+            mix(tick)
+        for c in range(CHUNKS):
+            if 0 <= tick - c - 1 < ZN:
+                relay(c, tick - c - 1)
+        for c in range(CHUNKS):
+            if 1 <= tick - c + 1 < ZN:
+                step(c, tick - c + 1)
+        if tick == CHUNKS + 1:
+            swaps[3][0]()
     for copy in places:
         copy.wait()
     for c in range(CHUNKS):
@@ -399,20 +415,19 @@
         del refs[:n]
         return got
 
-    (lengths, pick, gates, w_kv) = take(4)
+    (lengths, ids, gates, w_kv, prompt_rows) = take(5)
     w_parts = take(3)
-    (outgoing,) = take(1)
     latents = take(4)
     outs = take(3)
     heads = take(4)
     kv, rows = take(2)
-    encode_scratch = take(8)
+    encode_scratch = take(11)
     encode_sems = take(7)
     wsems = take(11)
     msems = take(11)
     greet(["seq", "lang"])
     encode(
-        w_parts, outgoing, pick, gates, w_kv, latents, heads, kv, rows,
+        w_parts, prompt_rows, ids, gates, w_kv, latents, heads, kv, rows,
         *encode_scratch, *encode_sems, wsems, msems,
     )
     q, k, v, g = heads
@@ -657,18 +672,13 @@
     ff = w_gate.shape[2]
     capacity = 3 * rows_local // experts_all
     sds = jax.ShapeDtypeStruct
-    targets = slot_targets(expert_ids, experts_all, capacity)
-    slot_ids = jnp.arange(experts_all * capacity, dtype=jnp.int32)
-    dispatch_mask = jnp.any(slot_ids[:, None, None] == targets[None, :, :], axis=2).astype(BF)
-    outgoing = jnp.dot(dispatch_mask, prompt_rows, preferred_element_type=F32).astype(BF)
-    outgoing = outgoing.reshape(experts_all, capacity, model_width)
-    pick = (targets.T[:, :, None] == slot_ids[None, None, :]).astype(BF)
     pages, part, _ = latent_q.shape
     lat = part * seq_count
     half = lang_count // 2
     chunk = model_width // half
     bq = lat // YN
     slots = experts_all * capacity
+    blocks = (experts_all, capacity, model_width)
     att_rows, latent, total = remote(
         whole_kernel,
         1,
@@ -681,13 +691,16 @@
         + [
             pltpu.VMEM((pages * lat, 2 * HD), BF),
             pltpu.VMEM((rows_local * seq_count, model_width), BF),
+            pltpu.VMEM((2, slots, rows_local), BF),
+            pltpu.VMEM((2, rows_local, rows_local), F32),
+            pltpu.VMEM(blocks, BF),
             pltpu.VMEM((3 * ff, model_width), BF),
-            pltpu.VMEM(outgoing.shape, BF),
+            pltpu.VMEM(blocks, BF),
             pltpu.VMEM((slots, model_width), BF),
             pltpu.VMEM((slots, 2 * ff), F32),
             pltpu.VMEM((slots, ff), BF),
-            pltpu.VMEM(outgoing.shape, BF),
-            pltpu.VMEM(outgoing.shape, BF),
+            pltpu.VMEM(blocks, BF),
+            pltpu.VMEM(blocks, BF),
             pltpu.VMEM((rows_local, model_width), BF),
             DMA((1, lang_count)),
             DMA((1, lang_count)),
@@ -724,18 +737,18 @@
             DMA((half,)),
         ],
         prompt_lengths,
-        pick,
-        expert_gates,
+        expert_ids.T,
+        expert_gates.T,
         w_kv.reshape(model_width, 2 * HD),
+        prompt_rows,
         w_gate[0].T,
         w_up[0].T,
         w_down[0],
-        outgoing,
         latent_q,
         latent_k,
         latent_v,
         grad_out,
-        in_vmem=(1, 2, 3),
+        in_vmem=(1, 2, 3, 4),
         in_smem=(0,),
     )
     grad_wkv = total.astype(F32).reshape(model_width, 2, HD)

time: 312 us -> 299 us (0.958)
  Pallas kernels: 297 us -> 290 us
    pallas_call x1, Pallas kernels: 297 us -> 290 us  [remote(): pl.pallas_call(body, out_shape=out_shape, in_specs=[pl.BlockSpec(memory_s...]
    unnamed x11 -> x7, local copies, waits for them, and re-layouts: 6.53 us -> 4.28 us
where the time goes in v5:
time: 299 us; the launch traced here: 298 us
  Pallas kernels  290 us (97%)
  local copies, waits for them, and re-layouts  7.47 us (2%)
    pallas_call x1, Pallas kernels, remote(): pl.pallas_call(body, out_shape=out_shape, in_specs=[pl.BlockSpec(memory_s...  290 us

profile of v5, /device:TPU:1, one launch (start us, length us, event | category | flops | bytes accessed | tf_op | source)
XLA Modules:
  0.0 298.1 jit_solution(12211028288688909119)
XLA Ops:
  0.6 2.3 copy.17
  3.0 290.0 %shard_map.139 = (bf16[2,64,2048]{2,1,0:T(8,128)(2,1)}, bf16[3,2,64,2048]{3,2,1,0:T(8,128)(2,1)}, bf16[2048,256]{1,0:T(8,128)(2,1)}) custom-call(s32[2]{0:T(128)} %refs_0_.1, s32[2,128]{1,0:T(2,128)} %bitcast.18, f32[2,128]{1,0:T(2,128)} %bitcast.19, bf16[2048,256]{1,0:T(8,128)(2,1)} %bitcast.13, bf16[128,2048]{1,0:T(8,128)(2,1)} %refs_4_.1, ...), custom_call_target="tpu_custom_call" | custom-call | tf_op jit(solution)/shard_map/pallas_call | solution.py:635
  293.0 0.0 copy-start.1
  293.0 0.0 copy-start
  293.0 3.2 %reshape.19 = f32[2048,2,128]{2,1,0:T(2,128)} reshape(bf16[2048,256]{1,0:T(8,128)(2,1)} %get-tuple-element.8) | data formatting | bytes 3145728 | tf_op jit(solution)/shard_map/reshape | solution.py:754
  296.2 0.0 copy-done.1
  296.2 0.8 copy.20
  297.0 0.0 copy-done
  297.0 1.1 copy.21
Async XLA Ops:
  293.0 3.2 %copy-start.1 = (bf16[2,64,2048]{2,1,0:T(8,128)(2,1)S(1)}, bf16[2,64,2048]{2,1,0:T(8,128)(2,1)}, u32[]{:S(2)}) copy-start(bf16[2,64,2048]{2,1,0:T(8,128)(2,1)} %get-tuple-element.12) | copy-start | bytes 1572868
  293.0 4.0 %copy-start = (bf16[3,2,64,2048]{3,2,1,0:T(8,128)(2,1)S(1)}, bf16[3,2,64,2048]{3,2,1,0:T(8,128)(2,1)}, u32[]{:S(2)}) copy-start(bf16[3,2,64,2048]{3,2,1,0:T(8,128)(2,1)} %get-tuple-element.13) | copy-start | bytes 4718596

commit v6 on v5

--- a/solution.py
+++ b/solution.py
@@ -236,8 +236,8 @@
 
 
 def encode(
-    w_parts, prompt_rows, ids, gates, w_kv, latents, heads, kv, rows,
-    masks, gate_columns, outgoing, whole, arrived, tokens, gate_up, hidden, results, returned, mixed,
+    w_parts, prompt_rows, ids, gates, w_kv, latents, heads, kv, rows, kv_sum,
+    w_flat, masks, gate_columns, outgoing, whole, arrived, tokens, gate_up, hidden, results, returned, mixed,
     dsend, drecv, rsend, rrecv, lsend, lrecv, own_sem, wsems, msems,
 ):
     s = lax.axis_index("seq")
@@ -309,6 +309,15 @@
             swaps[2][0]()
     for c in range(3):
         wrelay(c, ZN - 1)
+
+    def one_split(i, carry):
+        at = pl.ds(pl.multiple_of(i * 256, 256), 256)
+        both = w_kv[at, :, :].astype(F32)
+        w_flat[at, pl.ds(0, HD)] = both[:, 0, :].astype(BF)
+        w_flat[at, pl.ds(HD, HD)] = both[:, 1, :].astype(BF)
+        return carry
+
+    lax.fori_loop(0, width // 256, one_split, 0)
     dfinish()
     for copy in own:
         copy.wait()
@@ -393,12 +402,19 @@
     for c in range(CHUNKS):
         landed(c)
 
-    def one_part(i, carry):
-        at = pl.ds(pl.multiple_of(i * 256, 256), 256)
-        kv[at, :] = jnp.dot(rows[at, :], w_kv[...], preferred_element_type=F32).astype(BF)
-        return carry
-
-    lax.fori_loop(0, rows.shape[0] // 256, one_part, 0)
+        def one_part(i, carry):
+            at = pl.ds(pl.multiple_of(i * 256, 256), 256)
+            depth = pl.ds(c * wide, wide)
+            part = jnp.dot(rows[at, depth], w_flat[depth, :], preferred_element_type=F32)
+            if c > 0:
+                part = part + kv_sum[at, :]
+            if c < CHUNKS - 1:
+                kv_sum[at, :] = part
+            else:
+                kv[at, :] = part.astype(BF)
+            return carry
+
+        lax.fori_loop(0, rows.shape[0] // 256, one_part, 0)
     for swap in swaps:
         swap[1]()
     for c in range(3):
@@ -421,13 +437,13 @@
     outs = take(3)
     heads = take(4)
     kv, rows = take(2)
-    encode_scratch = take(11)
+    encode_scratch = take(12)
     encode_sems = take(7)
     wsems = take(11)
     msems = take(11)
     greet(["seq", "lang"])
     encode(
-        w_parts, prompt_rows, ids, gates, w_kv, latents, heads, kv, rows,
+        w_parts, prompt_rows, ids, gates, w_kv, latents, heads, kv, rows, refs[9],
         *encode_scratch, *encode_sems, wsems, msems,
     )
     q, k, v, g = heads
@@ -589,7 +605,6 @@
         return carry
 
     lax.fori_loop(1, group, one_part, 0)
-    send_key_grads(pages - 1)
     own = []
     for i in range(4):
         own.append(
@@ -609,6 +624,7 @@
         mine, pair, psend.at[0], precv.at[0], "lang", lax.rem(l + group, 2 * group)
     )
     cross.start()
+    send_key_grads(pages - 1)
     cross.wait()
     done[...] = (mine[...].astype(F32) + pair[...].astype(F32)).T.astype(BF)
     for k in range(1, group):
@@ -691,6 +707,7 @@
         + [
             pltpu.VMEM((pages * lat, 2 * HD), BF),
             pltpu.VMEM((rows_local * seq_count, model_width), BF),
+            pltpu.VMEM((model_width, 2 * HD), BF),
             pltpu.VMEM((2, slots, rows_local), BF),
             pltpu.VMEM((2, rows_local, rows_local), F32),
             pltpu.VMEM(blocks, BF),
@@ -739,7 +756,7 @@
         prompt_lengths,
         expert_ids.T,
         expert_gates.T,
-        w_kv.reshape(model_width, 2 * HD),
+        w_kv,
         prompt_rows,
         w_gate[0].T,
         w_up[0].T,

time: 299 us -> 296 us (0.990)
  Pallas kernels: 290 us -> 287 us
    pallas_call x1, Pallas kernels: 290 us -> 287 us  [remote(): pl.pallas_call(body, out_shape=out_shape, in_specs=[pl.BlockSpec(memory_s...]
where the time goes in v6:
time: 296 us; the launch traced here: 292 us
  Pallas kernels  287 us (97%)
  local copies, waits for them, and re-layouts  5.14 us (2%)
    pallas_call x1, Pallas kernels, remote(): pl.pallas_call(body, out_shape=out_shape, in_specs=[pl.BlockSpec(memory_s...  287 us

profile of v6, /device:TPU:1, one launch (start us, length us, event | category | flops | bytes accessed | tf_op | source)
XLA Modules:
  0.0 292.4 jit_solution(2566080607331455440)
XLA Ops:
  0.6 286.6 %shard_map.139 = (bf16[2,64,2048]{2,1,0:T(8,128)(2,1)}, bf16[3,2,64,2048]{3,2,1,0:T(8,128)(2,1)}, bf16[2048,256]{1,0:T(8,128)(2,1)}) custom-call(s32[2]{0:T(128)} %refs_0_.1, s32[2,128]{1,0:T(2,128)} %bitcast.12, f32[2,128]{1,0:T(2,128)} %bitcast.13, bf16[2048,2,128]{2,1,0:T(2,128)(2,1)} %refs_3_.1, bf16[128,2048]{1,0:T(8,128)(2,1)} %refs_4_.1, ...), custom_call_target="tpu_custom_call" | custom-call | tf_op jit(solution)/shard_map/pallas_call | solution.py:651
  287.3 0.0 copy-start.1
  287.3 0.0 copy-start
  287.3 3.2 %reshape.15 = f32[2048,2,128]{2,1,0:T(2,128)} reshape(bf16[2048,256]{1,0:T(8,128)(2,1)} %get-tuple-element.8) | data formatting | bytes 3145728 | tf_op jit(solution)/shard_map/reshape | solution.py:771
  290.5 0.0 copy-done.1
  290.5 0.8 copy.17
  291.3 0.0 copy-done
  291.3 1.1 copy.18
Async XLA Ops:
  287.3 3.2 %copy-start.1 = (bf16[2,64,2048]{2,1,0:T(8,128)(2,1)S(1)}, bf16[2,64,2048]{2,1,0:T(8,128)(2,1)}, u32[]{:S(2)}) copy-start(bf16[2,64,2048]{2,1,0:T(8,128)(2,1)} %get-tuple-element.12) | copy-start | bytes 1572868
  287.3 4.0 %copy-start = (bf16[3,2,64,2048]{3,2,1,0:T(8,128)(2,1)S(1)}, bf16[3,2,64,2048]{3,2,1,0:T(8,128)(2,1)}, u32[]{:S(2)}) copy-start(bf16[3,2,64,2048]{3,2,1,0:T(8,128)(2,1)} %get-tuple-element.13) | copy-start | bytes 4718596
